TPU v7x, 128 devices: a whole 4x4x4 slice. The times are simulated.
128 devices in a mesh: pair: 16 (over z, x), slab: 8 (over y, core).
Axes of the slice: x: 4, y: 4, z: 4, core: 2. Of those that a mesh axis runs over, the one named last changes fastest.
Arguments:
- amplitudes: bfloat16 [16, 8, 512, 512], P('pair', 'slab'), may hold values from -6 to 6
- integrals: bfloat16 [8, 16, 512, 512], P(None, 'pair', 'slab'), may hold values from -0.25 to 0.25
- occ_irrep: int32 [16, 1], replicated, may hold values from 0 to 7
- slab_irrep: int32 [8], replicated, may hold values from 0 to 7, each once
- virt_irrep: int32 [512, 1], replicated, may hold values from 0 to 7
Outputs:
- residual: float32 [16, 16, 512, 512], P('pair', None, 'slab')
Inputs may be any that keep to these rules, and one draw needn't show every extreme that they name: `occ_irrep`: D2h irrep labels; the product of two irreps is the bitwise exclusive or of their labels; every label appears among the 16 window orbitals, among the 512 virtuals, and exactly once among the 8 slab orbitals.
All inputs are finite; a program needn't handle non-finite values.
Results may differ from a plain program's by a relative error of at most 0.0003.
Values may be sent and summed in bfloat16 or wider, within the bound.
A program may use at most 64 MiB of HBM per device.

v0:
```python
import jax
import jax.numpy as jnp
from jax import lax
from jax.sharding import PartitionSpec as P


def apply_mask(values, own_irrep, slab_labels, virt_pairs):
    occ_slab = jnp.bitwise_xor(own_irrep[:, None], slab_labels[None, :])
    allowed = occ_slab[:, :, None, None] == virt_pairs[None, None, :, :]
    return values * allowed.astype(values.dtype)


def local(amplitudes, integrals, occ_irrep, slab_irrep, virt_irrep):
    own_rows = amplitudes.shape[0]
    row_start = lax.axis_index("pair") * own_rows
    own_irrep = lax.dynamic_slice_in_dim(occ_irrep[:, 0], row_start, own_rows, 0)
    virt_labels = virt_irrep[:, 0]
    virt_pairs = jnp.bitwise_xor(virt_labels[:, None], virt_labels[None, :])
    own_tile = integrals.shape[2]
    tile_start = lax.axis_index("slab") * own_tile
    tile_labels = lax.dynamic_slice_in_dim(virt_labels, tile_start, own_tile, 0)
    tile_pairs = jnp.bitwise_xor(tile_labels[:, None], virt_labels[None, :])
    slab_occ = jnp.bitwise_xor(slab_irrep[:, None], own_irrep[None, :])
    int_allowed = slab_occ[:, :, None, None] == tile_pairs[None, None, :, :]
    sym_ints = integrals * int_allowed.astype(integrals.dtype)
    gathered = lax.all_gather(amplitudes, "slab", axis=1, tiled=True)
    sym_amps = apply_mask(gathered, own_irrep, slab_irrep, virt_pairs)
    cycle_term = jnp.einsum(
        "ikac,kjbc->ijba",
        sym_amps,
        lax.all_gather(sym_ints, "pair", axis=1, tiled=True),
        preferred_element_type=jnp.float32,
    )
    occ_count = cycle_term.shape[1]
    tile_width = cycle_term.shape[2]
    virt_count = cycle_term.shape[3]
    pair_count = lax.axis_size("pair")
    slab_count = lax.axis_size("slab")
    blocked = cycle_term.reshape(own_rows, pair_count, own_rows, tile_width, slab_count, tile_width)
    blocked = jnp.transpose(blocked, (1, 4, 0, 2, 3, 5))
    blocked = blocked.reshape(pair_count * slab_count, own_rows, own_rows, tile_width, tile_width)
    exchanged = lax.all_to_all(blocked, ("pair", "slab"), split_axis=0, concat_axis=0, tiled=True)
    exchanged = exchanged.reshape(
        pair_count, slab_count, own_rows, own_rows, tile_width, tile_width
    )
    mirrored = jnp.transpose(exchanged, (3, 0, 2, 5, 1, 4))
    mirrored = mirrored.reshape(own_rows, occ_count, tile_width, virt_count)
    return cycle_term + mirrored


def solution(mesh):
    placed = (P("pair", "slab", None, None), P(None, "pair", "slab", None), P(), P(), P())
    return jax.shard_map(
        local, mesh=mesh, in_specs=placed, out_specs=P("pair", None, "slab", None), check_vma=False
    )
```

profile of v0, /device:TPU:0, one launch (start us, length us, event | category | flops | bytes accessed | tf_op | source)
XLA Modules:
  0.0 204.7 jit_solution(7343294543206884851)
XLA Ops:
  6.5 0.0 copy-start
  6.5 0.0 all-gather.5.cloned.1.call-start
  6.5 0.7 all-gather.5.cloned.1.call-update
  7.3 0.0 all-gather.3.cloned.1.call-start
  7.3 0.0 copy-done
  7.3 0.6 constant_dynamic-slice_fusion
  7.9 0.7 dynamic-slice_bitcast_fusion
  8.6 1.3 broadcast_xor_fusion.2
  9.9 0.8 broadcast_xor_fusion.1
  10.7 2.0 compare_select_fusion.1
  12.7 0.0 all-gather.3.cloned.1.call-update
  12.7 0.9 broadcast_xor_fusion
  13.6 30.1 %all-gather.5.cloned.1.call-done = bf16[1,8,512,512]{3,2,0,1:T(8,128)(2,1)} async-done(((bf16[1,1,512,512]{3,2,0,1:T(8,128)(2,1)}), bf16[1,8,512,512]{3,2,0,1:T(8,128)(2,1)}) %all-gather.5.cloned.1.call-update) | async-done | bytes 4194320 | tf_op jit(solution)/shard_map/all_gather | solution.py:26
  43.7 73.0 %all-gather.3.cloned.1.call-done = bf16[8,16,64,512]{3,2,0,1:T(8,128)(2,1)} async-done(((bf16[8,1,64,512]{3,2,0,1:T(8,128)(2,1)}), bf16[8,16,64,512]{3,2,0,1:T(8,128)(2,1)}) %all-gather.3.cloned.1.call-update) | async-done | bytes 8388624 | tf_op jit(solution)/shard_map/all_gather | solution.py:31
  116.7 8.7 %fusion.6 = f32[16,64,512]{2,1,0:T(8,128)S(1)} fusion(bf16[8,16,64,512]{3,2,0,1:T(8,128)(2,1)} %all-gather.3.cloned.1.call-done, bf16[1,8,512,512]{3,2,0,1:T(8,128)(2,1)} %all-gather.5.cloned.1.call-done, s32[512,512]{1,0:T(8,128)S(1)} %broadcast_xor_fusion, s32[8]{0:T(128)S(1)} %broadcast_xor_fusion.2), kind=kOutput, calls=%fused_computation.7 | convolution fusion | flops 4299161600 | bytes 15728672 | tf_op jit(solution)/shard_map/ikac,kjbc->ijba/dot_general | solution.py:28
  125.4 2.4 %transpose.18 = f32[1,16,1,64,8,64]{5,4,3,1,2,0:T(8,128)} reshape(f32[16,64,512]{2,1,0:T(8,128)S(1)} %fusion.6) | data formatting | bytes 4194304 | tf_op jit(solution)/shard_map/reshape;ikac,kjbc->ijba/transpose | solution.py:39
  127.8 4.9 %copy.12 = f32[1,16,1,64,8,64]{5,3,4,1,2,0:T(8,128)} copy(f32[1,16,1,64,8,64]{5,4,3,1,2,0:T(8,128)} %transpose.18) | data formatting | bytes 4194304 | tf_op jit(solution)/shard_map/reshape;ikac,kjbc->ijba/transpose | solution.py:39
  132.7 5.5 %reshape.116 = f32[128,1,4096]{2,1,0:T(1,128)} reshape(f32[128,1,1,64,64]{4,3,2,1,0:T(8,128)} %bitcast.30) | data formatting | bytes 4194304
  138.2 38.7 %all_to_all.5 = f32[128,1,4096]{2,1,0:T(1,128)} all-to-all(f32[128,1,4096]{2,1,0:T(1,128)} %reshape.116), channel_id=1, replica_groups=mesh['pair'=16,'slab'=8] {'pair','slab'}, dimensions={0} | all-to-all | bytes 4194304 | tf_op jit(solution)/shard_map/all_to_all | solution.py:42
  176.9 0.5 broadcast.91
  177.4 8.6 %reduce = f32[128,4096]{1,0:T(8,128)} reduce(f32[128,1,4096]{2,1,0:T(1,128)} %all_to_all.5, f32[]{:T(128)} %broadcast.91), dimensions={1}, to_apply=%all_to_all.3.reduce_sub_computation | reduce | bytes 4194308 | tf_op jit(solution)/shard_map/all_to_all | solution.py:42
  186.0 4.6 %reshape.117 = f32[128,1,1,64,64]{4,3,2,1,0:T(8,128)} reshape(f32[128,4096]{1,0:T(8,128)} %reduce) | data formatting | bytes 4194304
  190.6 3.8 %copy.16 = f32[16,64,512]{2,1,0:T(8,128)} copy(f32[16,64,512]{1,2,0:T(8,128)} %bitcast.29) | data formatting | bytes 4194304 | tf_op jit(solution)/shard_map/reshape | solution.py:47
  194.4 3.5 %add_bitcast_fusion = f32[1,16,64,512]{3,2,1,0:T(8,128)} fusion(f32[16,64,512]{2,1,0:T(8,128)S(1)} %fusion.6, f32[16,64,512]{2,1,0:T(8,128)} %copy.16), kind=kLoop, calls=%fused_computation.5 | loop fusion | flops 524288 | bytes 6291456 | tf_op jit(solution)/shard_map/add | solution.py:48
Async XLA Ops:
  6.5 0.8 copy-start
  6.5 37.2 %all-gather.5.cloned.1.call-start = ((), (), s32[]{:S(2)}) async-start(), calls=%async_computation.2 | async-start | bytes 4718592 | tf_op jit(solution)/shard_map/all_gather | solution.py:26
  7.3 109.4 %all-gather.3.cloned.1.call-start = ((), (), s32[]{:S(2)}) async-start(), calls=%async_computation.1 | async-start | bytes 8912896 | tf_op jit(solution)/shard_map/all_gather | solution.py:31
Sparse Core Ops, SparseCore 0:
  9.1 34.5 all-gather.4
  45.8 70.7 all-gather.2
where the time goes:
time: 206 us; the launch traced here: 205 us
  waiting for transfers between devices  104 us (50%)
  blocking collectives  38.7 us (19%)
  local copies, waits for them, and re-layouts  23 us (11%)
  other arithmetic  17.1 us (8%)
  between operations  13.4 us (7%)
  matrix products  8.72 us (4%)
    all_gather x1, waiting for transfers between devices, local(): lax.all_gather(sym_ints, 'pair', axis=1, tiled=True)  73 us
    all_to_all x1, blocking collectives, local(): lax.all_to_all(blocked, ('pair', 'slab'), split_axis=0, concat_axis=0, ti...  38.7 us
    all_gather x1, waiting for transfers between devices, local(): gathered = lax.all_gather(amplitudes, 'slab', axis=1, tiled=True)  30.1 us
    unnamed x4, local copies, waits for them, and re-layouts  10.1 us
    dot_general x1, matrix products, local(): jnp.einsum('ikac,kjbc->ijba', sym_amps, lax.all_gather(sym_ints, 'pair',...  8.72 us
    all_to_all x1, other arithmetic, local(): lax.all_to_all(blocked, ('pair', 'slab'), split_axis=0, concat_axis=0, ti...  8.61 us
    transpose x2, local copies, waits for them, and re-layouts, local(): cycle_term.reshape(own_rows, pair_count, own_rows, tile_width, slab_count...  7.27 us
  transfers between devices with their start and end apart: 2, of which 2 were waited for; matrix products, arithmetic and copies ran while one was open for 3% of the time, Pallas kernels for 0%

commit v1 on v0

v1 whole, which is shorter than its diff:
```python
import jax
import jax.numpy as jnp
from jax import lax
from jax.experimental import pallas as pl
from jax.experimental.pallas import tpu as pltpu
from jax.sharding import PartitionSpec as P

NX = NY = NZ = 4
NJ = 16
NS = 8
TILE = 64
V = 512
N_SEMS = 96
BF16 = jnp.bfloat16
F32 = jnp.float32


def wrap(at, step, size):
    return lax.rem(at + step + size, size)


def kernel(
    amps_hbm, ints_hbm, occ_ref, slab_ref, virt_ref, out_ref,
    amps, ints, row_labels, to_sibling, from_sibling, part, from_ring,
    pair_w, pair_a, slab_w, slab_a, load_sems, send_sems, recv_sems,
):
    pair, slab = lax.axis_index("pair"), lax.axis_index("slab")
    z, x = pair // NX, lax.rem(pair, NX)
    y, core = slab // 2, lax.rem(slab, 2)
    sibling_core = 1 - core

    def at_pair(dz, dx):
        return wrap(z, dz, NZ) * NX + wrap(x, dx, NX)

    def at_slab(dy, own_core=True):
        return wrap(y, dy, NY) * 2 + (core if own_core else sibling_core)

    device = {
        "x+": (at_pair(0, 1), slab), "x-": (at_pair(0, -1), slab),
        "z+": (at_pair(1, 0), slab), "z-": (at_pair(-1, 0), slab),
        "y+": (pair, at_slab(1)), "y-": (pair, at_slab(-1)),
        "sibling": (pair, at_slab(0, False)),
    }

    load_amps = pltpu.make_async_copy(amps_hbm.at[0, 0], amps, load_sems.at[0])
    load_ints = pltpu.make_async_copy(ints_hbm.at[:, 0], ints, load_sems.at[1])
    load_amps.start()
    load_ints.start()

    barrier = pltpu.get_barrier_semaphore()
    for to in device.values():
        pl.semaphore_signal(barrier, inc=1, device_id=to, device_id_type=pl.DeviceIdType.MESH)

    started, order = [], {}

    def copy(name, src, dst, to):
        at = order.setdefault(name, len(order))
        return pltpu.make_async_remote_copy(
            src_ref=src, dst_ref=dst, send_sem=send_sems.at[at], recv_sem=recv_sems.at[at],
            device_id=device[to], device_id_type=pl.DeviceIdType.MESH,
        )

    def send(name, src, dst, to):
        sent = copy(name, src, dst, to)
        sent.start()
        started.append(sent)

    def arrive(name, dst, to):
        copy(name, dst, dst, to).wait_recv()

    columns = virt_ref[...]
    for at in range(V // 128):
        lanes = jnp.broadcast_to(columns[:, at * 128 : (at + 1) * 128], (128, 128))
        row_labels[at * 128 : (at + 1) * 128, :] = lanes.T

    def pair_labels(tile):
        rows = row_labels[pl.ds(pl.multiple_of(tile * TILE, TILE), TILE), :]
        return jnp.concatenate([rows] * (V // 128), axis=1) ^ columns

    own_label = occ_ref[pair]
    amps_label = own_label ^ slab_ref[slab]

    def masked(tile):
        block = amps[pl.ds(pl.multiple_of(tile * TILE, TILE), TILE), :].astype(F32)
        chosen = jnp.where(pair_labels(tile) == amps_label, block, 0.0)
        return chosen.astype(BF16).reshape(2, 2, 16, V)

    load_amps.wait()
    for at in range(NY):
        to_sibling[at] = masked(2 * at + sibling_core)

    pl.semaphore_wait(barrier, len(device))
    send("merge", to_sibling, from_sibling, "sibling")

    load_ints.wait()
    wanted = pair_labels(slab) ^ own_label
    w = jnp.zeros((TILE, V), F32)
    for k in range(8):
        w = jnp.where(wanted == slab_ref[k], ints[k].astype(F32), w)
    w = w.astype(BF16).reshape(2, 2, 16, V)
    pair_w[pair] = w
    slab_w[slab] = w

    def pair_start(tag, buf):
        for to in ("x+", "x-", "z+", "z-"):
            send(tag + to, buf.at[pair], buf.at[pair], to)

    def pair_near(tag, buf):
        for axis, other, half in (("x", "z", 0), ("z", "x", 1)):
            for came, step, on, quarter in (("-", -1, "+", 0), ("+", 1, "-", 1)):
                at = at_pair(0, step) if axis == "x" else at_pair(step, 0)
                arrive(tag + axis + on, buf.at[at], axis + on)
                send(tag + "far" + axis + on, buf.at[at, :, quarter], buf.at[at, :, quarter], axis + on)
                for way in ("+", "-"):
                    send(tag + "turn" + axis + came + other + way, buf.at[at, half], buf.at[at, half], other + way)

    def pair_middle(tag, buf):
        for axis, other, half in (("x", "z", 0), ("z", "x", 1)):
            at = at_pair(0, 2) if axis == "x" else at_pair(2, 0)
            for on, quarter in (("+", 0), ("-", 1)):
                arrive(tag + "far" + axis + on, buf.at[at, :, quarter], axis + on)
            for way in ("+", "-"):
                send(tag + "turn" + axis + "2" + other + way, buf.at[at, half], buf.at[at, half], other + way)
        for axis, other, half in (("x", "z", 0), ("z", "x", 1)):
            for turn, side in (("-", -1), ("+", 1)):
                for step, way, quarter in ((-1, "+", 0), (1, "-", 1)):
                    at = at_pair(step, side) if axis == "x" else at_pair(side, step)
                    arrive(tag + "turn" + axis + turn + other + way, buf.at[at, half], other + way)
                    piece = buf.at[at, half, quarter]
                    send(tag + "last" + axis + turn + other + way, piece, piece, other + way)

    def pair_far(tag, buf):
        for axis, other, half in (("x", "z", 0), ("z", "x", 1)):
            for step, way, quarter in ((-1, "+", 0), (1, "-", 1)):
                at = at_pair(step, 2) if axis == "x" else at_pair(2, step)
                arrive(tag + "turn" + axis + "2" + other + way, buf.at[at, half], other + way)
                piece = buf.at[at, half, quarter]
                send(tag + "last" + axis + "2" + other + way, piece, piece, other + way)
        for axis, other, half in (("x", "z", 0), ("z", "x", 1)):
            for turn, side in (("-", -1), ("+", 1)):
                at = at_pair(2, side) if axis == "x" else at_pair(side, 2)
                for way, quarter in (("+", 0), ("-", 1)):
                    arrive(tag + "last" + axis + turn + other + way, buf.at[at, half, quarter], other + way)

    def pair_end(tag, buf):
        at = at_pair(2, 2)
        for axis, other, half in (("x", "z", 0), ("z", "x", 1)):
            for way, quarter in (("+", 0), ("-", 1)):
                arrive(tag + "last" + axis + "2" + other + way, buf.at[at, half, quarter], other + way)

    def slab_start(tag, buf):
        for to in ("y+", "y-", "sibling"):
            send(tag + to, buf.at[slab], buf.at[slab], to)

    def slab_near(tag, buf):
        for step, on, half in ((-1, "+", 0), (1, "-", 1)):
            at = at_slab(step)
            arrive(tag + "y" + on, buf.at[at], "y" + on)
            send(tag + "far" + on, buf.at[at, half], buf.at[at, half], "y" + on)
            send(tag + "over" + on, buf.at[at], buf.at[at], "sibling")

    def slab_far(tag, buf):
        at = at_slab(2)
        for on, half in (("+", 0), ("-", 1)):
            arrive(tag + "far" + on, buf.at[at, half], "y" + on)
        send(tag + "over2", buf.at[at], buf.at[at], "sibling")

    def slab_end(tag, buf):
        arrive(tag + "sibling", buf.at[at_slab(0, False)], "sibling")
        arrive(tag + "over+", buf.at[at_slab(-1, False)], "sibling")
        arrive(tag + "over-", buf.at[at_slab(1, False)], "sibling")
        arrive(tag + "over2", buf.at[at_slab(2, False)], "sibling")

    pair_start("pw", pair_w)
    slab_start("sw", slab_w)

    for at in range(NY):
        part[at] = masked(2 * at + core)
    arrive("merge", from_sibling, "sibling")
    part[...] = part[...] + from_sibling[...]

    up, down, across = wrap(y, 1, NY), wrap(y, -1, NY), wrap(y, 2, NY)
    send("ring far+", part.at[across, 0], from_ring.at[0], "y+")
    send("ring far-", part.at[across, 1], from_ring.at[1], "y-")
    send("ring now+", part.at[up, 1], from_ring.at[2], "y+")
    send("ring now-", part.at[down, 0], from_ring.at[3], "y-")

    pair_near("pw", pair_w)

    arrive("ring far+", from_ring.at[0], "y+")
    part[up, 0] = part[up, 0] + from_ring[0]
    send("ring late+", part.at[up, 0], from_ring.at[4], "y+")
    arrive("ring far-", from_ring.at[1], "y-")
    part[down, 1] = part[down, 1] + from_ring[1]
    send("ring late-", part.at[down, 1], from_ring.at[5], "y-")

    slab_near("sw", slab_w)
    pair_middle("pw", pair_w)

    arrive("ring now+", from_ring.at[2], "y+")
    arrive("ring now-", from_ring.at[3], "y-")
    arrive("ring late+", from_ring.at[4], "y+")
    arrive("ring late-", from_ring.at[5], "y-")
    first = part[y, 0] + from_ring[3] + from_ring[4]
    second = part[y, 1] + from_ring[2] + from_ring[5]
    for half, value in ((0, first), (1, second)):
        pair_a[pair, half] = value
        slab_a[slab, half] = value
    slab_start("sa", slab_a)
    pair_start("pa", pair_a)

    slab_far("sw", slab_w)
    pair_far("pw", pair_w)
    slab_near("sa", slab_a)
    pair_near("pa", pair_a)
    slab_end("sw", slab_w)
    pair_end("pw", pair_w)
    slab_far("sa", slab_a)
    pair_middle("pa", pair_a)
    slab_end("sa", slab_a)

    def times(rows, every):
        return lax.dot_general(rows, every, (((1,), (1,)), ((), ())), preferred_element_type=F32)

    def first_term(at, n):
        every_a = slab_a[...].reshape(V, V)
        rows = pair_w[pl.ds(at, n)].reshape(n * TILE, V)
        out_ref[0, pl.ds(at, n)] = times(rows, every_a).reshape(n, TILE, V)

    def second_term(j):
        every_w = slab_w[...].reshape(V, V)
        term = times(pair_a[j].reshape(TILE, V), every_w)
        kept = pair_labels(slab) == (own_label ^ occ_ref[j])
        out_ref[0, j] = jnp.where(kept, out_ref[0, j] + term, 0.0)

    @pl.loop(0, NJ // 4)
    def _(at):
        first_term(at * 4, 4)

    pair_far("pa", pair_a)
    pair_end("pa", pair_a)

    @pl.loop(0, NJ)
    def _(j):
        second_term(j)

    for sent in started:
        sent.wait_send()


def solution(mesh):
    placed = (P("pair", "slab", None, None), P(None, "pair", "slab", None), P(), P(), P())
    piece = (2, 2, 16, V)

    def local(amplitudes, integrals, occ_irrep, slab_irrep, virt_irrep):
        vmem = pl.BlockSpec(memory_space=pltpu.VMEM)
        smem = pl.BlockSpec(memory_space=pltpu.SMEM)
        anywhere = pl.BlockSpec(memory_space=pl.ANY)
        return pl.pallas_call(
            kernel,
            out_shape=jax.ShapeDtypeStruct((1, NJ, TILE, V), F32),
            in_specs=[anywhere, anywhere, smem, smem, vmem],
            out_specs=vmem,
            scratch_shapes=[
                pltpu.VMEM((V, V), BF16),
                pltpu.VMEM((8, TILE, V), BF16),
                pltpu.VMEM((V, 128), jnp.int32),
                pltpu.VMEM((NY, *piece), BF16),
                pltpu.VMEM((NY, *piece), BF16),
                pltpu.VMEM((NY, *piece), BF16),
                pltpu.VMEM((6, 2, 16, V), BF16),
                pltpu.VMEM((NJ, *piece), BF16),
                pltpu.VMEM((NJ, *piece), BF16),
                pltpu.VMEM((NS, *piece), BF16),
                pltpu.VMEM((NS, *piece), BF16),
                pltpu.SemaphoreType.DMA((2,)),
                pltpu.SemaphoreType.DMA((N_SEMS,)),
                pltpu.SemaphoreType.DMA((N_SEMS,)),
            ],
            compiler_params=pltpu.CompilerParams(
                collective_id=0, has_side_effects=True, vmem_limit_bytes=32 * 1024 * 1024
            ),
        )(amplitudes, integrals, occ_irrep.reshape(NJ), slab_irrep, virt_irrep.reshape(1, V))

    return jax.shard_map(
        local, mesh=mesh, in_specs=placed, out_specs=P("pair", None, "slab", None), check_vma=False
    )
```

time: 206 us -> 43 us (0.21)
  waiting for transfers between devices: 104 us -> 0 us
  blocking collectives: 38.7 us -> 0 us
  Pallas kernels: 0 us -> 37.3 us
  local copies, waits for them, and re-layouts: 23 us -> 5.39 us
  other arithmetic: 17.1 us -> 0 us
  between operations: 13.4 us -> 0.01 us
  matrix products: 8.72 us -> 0 us
    all_gather x2 -> x0, waiting for transfers between devices: 103 us -> none  [the longest x1 73 us: local(): lax.all_gather(sym_ints, 'pair', axis=1, tiled=True)]
    all_to_all x1 -> x0, blocking collectives: 38.7 us -> none  [local(): lax.all_to_all(blocked, ('pair', 'slab'), split_axis=0, concat_axis=0, ti...]
    pallas_call x0 -> x1, Pallas kernels: none -> 37.3 us  [local(): pl.pallas_call(kernel, out_shape=jax.ShapeDtypeStruct((1, NJ, TILE, V), F...]
    dot_general x1 -> x0, matrix products: 8.72 us -> none  [local(): jnp.einsum('ikac,kjbc->ijba', sym_amps, lax.all_gather(sym_ints, 'pair',...]
    all_to_all x1 -> x0, other arithmetic: 8.61 us -> none  [local(): lax.all_to_all(blocked, ('pair', 'slab'), split_axis=0, concat_axis=0, ti...]
    transpose x2 -> x0, local copies, waits for them, and re-layouts: 7.27 us -> none  [local(): cycle_term.reshape(own_rows, pair_count, own_rows, tile_width, slab_count...]
    unnamed x4 -> x11, local copies, waits for them, and re-layouts: 10.1 us -> 5.39 us
    reshape x1 -> x0, local copies, waits for them, and re-layouts: 3.78 us -> none  [local(): mirrored = mirrored.reshape(own_rows, occ_count, tile_width, virt_count)]
  transfers between devices with their start and end apart: 2 -> 0, of which waited for: 2 -> 0; matrix products, arithmetic and copies ran while one was open for 3% -> 0% of each run, Pallas kernels for 0% -> 0%
where the time goes in v1:
time: 43 us; the launch traced here: 42.8 us
  Pallas kernels  37.3 us (87%)
  local copies, waits for them, and re-layouts  5.39 us (13%)
    pallas_call x1, Pallas kernels, local(): pl.pallas_call(kernel, out_shape=jax.ShapeDtypeStruct((1, NJ, TILE, V), F...  37.3 us
    unnamed x11, local copies, waits for them, and re-layouts  5.39 us

profile of v1, /device:TPU:0, one launch (start us, length us, event | category | flops | bytes accessed | tf_op | source)
XLA Modules:
  0.0 42.8 jit_solution(2764997656208403859)
XLA Ops:
  0.0 0.0 copy-start
  0.0 1.0 %copy-done = bf16[1,1,512,512]{3,2,1,0:T(8,128)(2,1)S(1)} copy-done((bf16[1,1,512,512]{3,2,1,0:T(8,128)(2,1)S(1)}, bf16[1,1,512,512]{3,2,1,0:T(8,128)(2,1)}, u32[]{:S(2)}) %copy-start) | copy-done | bytes 524312
  1.0 0.0 copy-start.1
  1.0 1.0 %copy-done.1 = bf16[8,1,64,512]{3,2,1,0:T(8,128)(2,1)S(1)} copy-done((bf16[8,1,64,512]{3,2,1,0:T(8,128)(2,1)S(1)}, bf16[8,1,64,512]{3,2,1,0:T(8,128)(2,1)}, u32[]{:S(2)}) %copy-start.1) | copy-done | bytes 524312
  2.1 0.0 copy-start.2
  2.1 0.7 %copy-done.2 = s32[512,1]{0,1:T(1,128)S(1)} copy-done((s32[512,1]{0,1:T(1,128)S(1)}, s32[512,1]{0,1:T(1,128)}, u32[]{:S(2)}) %copy-start.2) | copy-done | bytes 2072
  2.8 0.0 copy-start.3
  2.8 0.7 %copy-done.3 = s32[16,1]{0,1:T(1,128)S(1)} copy-done((s32[16,1]{0,1:T(1,128)S(1)}, s32[16,1]{0,1:T(1,128)}, u32[]{:S(2)}) %copy-start.3) | copy-done | bytes 88
  3.4 0.0 copy-start.4
  3.4 0.7 %copy-done.4 = s32[8]{0:T(128)S(1)} copy-done((s32[8]{0:T(128)S(1)}, s32[8]{0:T(128)}, u32[]{:S(2)}) %copy-start.4) | copy-done | bytes 56
  4.1 37.3 %shard_map.55 = f32[1,16,64,512]{3,2,1,0:T(8,128)S(1)} custom-call(bf16[1,1,512,512]{3,2,1,0:T(8,128)(2,1)S(1)} %copy-done, bf16[8,1,64,512]{3,2,1,0:T(8,128)(2,1)S(1)} %copy-done.1, s32[16]{0:T(128)S(1)} %bitcast.3, s32[8]{0:T(128)S(1)} %copy-done.4, s32[1,512]{1,0:T(1,128)S(1)} %bitcast.2), custom_call_target="tpu_custom_call" | custom-call | tf_op jit(solution)/shard_map/pallas_call | solution.py:259
  41.4 1.3 %copy.7 = f32[1,16,64,512]{3,2,1,0:T(8,128)} copy(f32[1,16,64,512]{3,2,1,0:T(8,128)S(1)} %shard_map.55) | data formatting | bytes 4194304
Async XLA Ops:
  0.0 1.0 %copy-start = (bf16[1,1,512,512]{3,2,1,0:T(8,128)(2,1)S(1)}, bf16[1,1,512,512]{3,2,1,0:T(8,128)(2,1)}, u32[]{:S(2)}) copy-start(bf16[1,1,512,512]{3,2,1,0:T(8,128)(2,1)} %amps_hbm.1) | copy-start | bytes 1572868
  1.0 1.0 %copy-start.1 = (bf16[8,1,64,512]{3,2,1,0:T(8,128)(2,1)S(1)}, bf16[8,1,64,512]{3,2,1,0:T(8,128)(2,1)}, u32[]{:S(2)}) copy-start(bf16[8,1,64,512]{3,2,1,0:T(8,128)(2,1)} %ints_hbm.1) | copy-start | bytes 1572868
  2.1 0.7 %copy-start.2 = (s32[512,1]{0,1:T(1,128)S(1)}, s32[512,1]{0,1:T(1,128)}, u32[]{:S(2)}) copy-start(s32[512,1]{0,1:T(1,128)} %param.9) | copy-start | bytes 6148
  2.8 0.7 %copy-start.3 = (s32[16,1]{0,1:T(1,128)S(1)}, s32[16,1]{0,1:T(1,128)}, u32[]{:S(2)}) copy-start(s32[16,1]{0,1:T(1,128)} %param.7) | copy-start | bytes 196
  3.4 0.7 %copy-start.4 = (s32[8]{0:T(128)S(1)}, s32[8]{0:T(128)}, u32[]{:S(2)}) copy-start(s32[8]{0:T(128)} %slab_ref.1) | copy-start | bytes 100

commit v2 on v0

v2 whole, which is shorter than its diff:
```python
import jax
import jax.numpy as jnp
from jax import lax
from jax.experimental import pallas as pl
from jax.experimental.pallas import tpu as pltpu
from jax.sharding import PartitionSpec as P

NX = NY = NZ = 4
NJ = 16
NS = 8
TILE = 64
V = 512
N_SEMS = 66
STEPS = (1, -1, 2)
BF16 = jnp.bfloat16
F32 = jnp.float32


def wrap(at, step, size):
    return lax.rem(at + step + size, size)


def kernel(
    amps_hbm, ints_hbm, occ_hbm, slab_hbm, virt_hbm, out_ref,
    amps, ints, occ_ref, slab_ref, virt_ref, row_labels, to_sibling, from_sibling, part, from_ring,
    pair_w, pair_a, slab_w, slab_a, load_sems, send_sems, recv_sems,
):
    pair, slab = lax.axis_index("pair"), lax.axis_index("slab")
    z, x = pair // NX, lax.rem(pair, NX)
    y, core = slab // 2, lax.rem(slab, 2)
    sibling_core = 1 - core

    def at_pair(dz, dx):
        return wrap(z, dz, NZ) * NX + wrap(x, dx, NX)

    def at_slab(dy, own_core=True):
        return wrap(y, dy, NY) * 2 + (core if own_core else sibling_core)

    device = {"sibling": (pair, at_slab(0, False))}
    for step in STEPS:
        device["x", step] = (at_pair(0, step), slab)
        device["z", step] = (at_pair(step, 0), slab)
        device["y", step] = (pair, at_slab(step))

    loads = [
        pltpu.make_async_copy(src, dst, load_sems.at[at])
        for at, (src, dst) in enumerate((
            (virt_hbm, virt_ref),
            (occ_hbm, occ_ref),
            (slab_hbm, slab_ref),
            (amps_hbm.at[:, sibling_core], amps.at[sibling_core]),
            (ints_hbm.at[:, 0], ints),
            (amps_hbm.at[:, core], amps.at[core]),
        ))
    ]
    for load in loads:
        load.start()

    barrier = pltpu.get_barrier_semaphore()
    for to in device.values():
        pl.semaphore_signal(barrier, inc=1, device_id=to, device_id_type=pl.DeviceIdType.MESH)

    started, order = [], {}

    def copy(name, src, dst, to):
        at = order.setdefault((name, to), len(order))
        return pltpu.make_async_remote_copy(
            src_ref=src, dst_ref=dst, send_sem=send_sems.at[at], recv_sem=recv_sems.at[at],
            device_id=device[to], device_id_type=pl.DeviceIdType.MESH,
        )

    def send(name, src, dst, to):
        sent = copy(name, src, dst, to)
        sent.start()
        started.append(sent)

    def arrive(name, dst, to):
        copy(name, dst, dst, to).wait_recv()

    for load in loads[:3]:
        load.wait()
    columns = virt_ref[...]
    for at in range(V // 128):
        lanes = jnp.broadcast_to(columns[:, at * 128 : (at + 1) * 128], (128, 128))
        row_labels[at * 128 : (at + 1) * 128, :] = lanes.T

    def pair_labels(tile):
        rows = row_labels[pl.ds(pl.multiple_of(tile * TILE, TILE), TILE), :]
        return jnp.concatenate([rows] * (V // 128), axis=1) ^ columns

    own_label = occ_ref[pair]
    amps_label = own_label ^ slab_ref[slab]

    def masked(at, of_core):
        block = amps[of_core, at].astype(F32)
        chosen = jnp.where(pair_labels(2 * at + of_core) == amps_label, block, 0.0)
        return chosen.astype(BF16).reshape(2, 2, 16, V)

    loads[3].wait()
    for at in range(NY):
        to_sibling[at] = masked(at, sibling_core)

    loads[4].wait()
    wanted = pair_labels(slab) ^ own_label
    w = jnp.zeros((TILE, V), F32)
    for k in range(8):
        w = jnp.where(wanted == slab_ref[k], ints[k].astype(F32), w)
    w = w.astype(BF16).reshape(2, 2, 16, V)
    pair_w[pair] = w
    slab_w[slab] = w

    axes = (("x", "z", 0), ("z", "x", 1))

    def beside(axis, step, other=0):
        return at_pair(other, step) if axis == "x" else at_pair(step, other)

    def pair_start(tag, buf):
        for step in STEPS:
            for axis in ("x", "z"):
                send(tag, buf.at[pair], buf.at[pair], (axis, step))

    def pair_turn(tag, buf):
        for step in STEPS:
            for axis, other, half in axes:
                at = beside(axis, -step)
                arrive(tag, buf.at[at], (axis, step))
                for way in STEPS:
                    send((tag, step), buf.at[at, half], buf.at[at, half], (other, way))

    def pair_end(tag, buf, step):
        for way in STEPS:
            for axis, other, half in axes:
                at = beside(axis, -step, -way) if axis == "x" else beside(axis, -way, -step)
                turned = step if axis == "x" else way
                sent = way if axis == "x" else step
                arrive((tag, turned), buf.at[at, half], (other, sent))

    def slab_start(tag, buf):
        for to in (("y", 1), ("y", -1), ("y", 2), "sibling"):
            send(tag, buf.at[slab], buf.at[slab], to)

    def slab_over(tag, buf):
        for step in STEPS:
            at = at_slab(-step)
            arrive(tag, buf.at[at], ("y", step))
            send((tag, step), buf.at[at], buf.at[at], "sibling")

    def slab_end(tag, buf):
        arrive(tag, buf.at[at_slab(0, False)], "sibling")
        for step in STEPS:
            arrive((tag, step), buf.at[at_slab(-step, False)], "sibling")

    pl.semaphore_wait(barrier, len(device))
    send("merge", to_sibling, from_sibling, "sibling")
    pair_start("pw", pair_w)
    slab_start("sw", slab_w)

    loads[5].wait()
    for at in range(NY):
        part[at] = masked(at, core)
    arrive("merge", from_sibling, "sibling")
    part[...] = part[...] + from_sibling[...]
    for at, step in enumerate(STEPS):
        send("ring", part.at[wrap(y, step, NY)], from_ring.at[at], ("y", step))

    pair_turn("pw", pair_w)
    slab_over("sw", slab_w)

    total = part[y]
    for at, step in enumerate(STEPS):
        arrive("ring", from_ring.at[at], ("y", step))
        total = total + from_ring[at]
    pair_a[pair] = total
    slab_a[slab] = total
    pair_start("pa", pair_a)
    slab_start("sa", slab_a)

    pair_turn("pa", pair_a)
    slab_over("sa", slab_a)
    for step in STEPS:
        pair_end("pw", pair_w, step)
    slab_end("sw", slab_w)
    slab_end("sa", slab_a)

    def times(rows, every):
        return lax.dot_general(rows, every, (((1,), (1,)), ((), ())), preferred_element_type=F32)

    @pl.loop(0, 2)
    def _(at):
        half = NJ // 2
        rows = pair_w[pl.ds(at * half, half)].reshape(half * TILE, V)
        out_ref[0, pl.ds(at * half, half)] = times(rows, slab_a[...].reshape(V, V)).reshape(half, TILE, V)

    labels = pair_labels(slab) ^ own_label

    def second_term(group):
        rows = jnp.concatenate([pair_a[j].reshape(TILE, V) for j in group], axis=0)
        term = times(rows, slab_w[...].reshape(V, V))
        for at, j in enumerate(group):
            both = out_ref[0, j] + term[at * TILE : (at + 1) * TILE]
            out_ref[0, j] = jnp.where(labels == occ_ref[j], both, 0.0)

    second_term([pair] + [beside(axis, step) for axis in ("x", "z") for step in STEPS])
    for step in STEPS:
        pair_end("pa", pair_a, step)
        second_term([beside("x", -step, -way) for way in STEPS])

    assert len(order) == N_SEMS
    for sent in started:
        sent.wait_send()


def solution(mesh):
    placed = (P("pair", "slab", None, None), P(None, "pair", "slab", None), P(), P(), P())
    piece = (2, 2, 16, V)

    def local(amplitudes, integrals, occ_irrep, slab_irrep, virt_irrep):
        operands = (
            amplitudes.reshape(NY, 2, TILE, V), integrals, occ_irrep.reshape(NJ), slab_irrep, virt_irrep.reshape(1, V)
        )
        return pl.pallas_call(
            kernel,
            out_shape=jax.ShapeDtypeStruct((1, NJ, TILE, V), F32),
            in_specs=[pl.BlockSpec(memory_space=pltpu.HBM)] * 5,
            out_specs=pl.BlockSpec(memory_space=pltpu.VMEM),
            scratch_shapes=[
                pltpu.VMEM((2, NY, TILE, V), BF16),
                pltpu.VMEM((8, TILE, V), BF16),
                pltpu.SMEM((NJ,), jnp.int32),
                pltpu.SMEM((8,), jnp.int32),
                pltpu.VMEM((1, V), jnp.int32),
                pltpu.VMEM((V, 128), jnp.int32),
                pltpu.VMEM((NY, *piece), BF16),
                pltpu.VMEM((NY, *piece), BF16),
                pltpu.VMEM((NY, *piece), BF16),
                pltpu.VMEM((3, *piece), BF16),
                pltpu.VMEM((NJ, *piece), BF16),
                pltpu.VMEM((NJ, *piece), BF16),
                pltpu.VMEM((NS, *piece), BF16),
                pltpu.VMEM((NS, *piece), BF16),
                pltpu.SemaphoreType.DMA((6,)),
                pltpu.SemaphoreType.DMA((N_SEMS,)),
                pltpu.SemaphoreType.DMA((N_SEMS,)),
            ],
            compiler_params=pltpu.CompilerParams(
                collective_id=0, has_side_effects=True, vmem_limit_bytes=32 * 1024 * 1024
            ),
        )(*(pltpu.with_memory_space_constraint(operand, pltpu.HBM) for operand in operands))

    return jax.shard_map(
        local, mesh=mesh, in_specs=placed, out_specs=P("pair", None, "slab", None), check_vma=False
    )
```

time: 206 us -> 28 us (0.14)
  waiting for transfers between devices: 104 us -> 0 us
  blocking collectives: 38.7 us -> 0 us
  Pallas kernels: 0 us -> 26.5 us
  local copies, waits for them, and re-layouts: 23 us -> 1.32 us
  other arithmetic: 17.1 us -> 0 us
  between operations: 13.4 us -> 0.01 us
  matrix products: 8.72 us -> 0 us
    all_gather x2 -> x0, waiting for transfers between devices: 103 us -> none  [the longest x1 73 us: local(): lax.all_gather(sym_ints, 'pair', axis=1, tiled=True)]
    all_to_all x1 -> x0, blocking collectives: 38.7 us -> none  [local(): lax.all_to_all(blocked, ('pair', 'slab'), split_axis=0, concat_axis=0, ti...]
    pallas_call x0 -> x1, Pallas kernels: none -> 26.5 us  [local(): pl.pallas_call(kernel, out_shape=jax.ShapeDtypeStruct((1, NJ, TILE, V), F...]
    unnamed x4 -> x1, local copies, waits for them, and re-layouts: 10.1 us -> 1.32 us
    dot_general x1 -> x0, matrix products: 8.72 us -> none  [local(): jnp.einsum('ikac,kjbc->ijba', sym_amps, lax.all_gather(sym_ints, 'pair',...]
    all_to_all x1 -> x0, other arithmetic: 8.61 us -> none  [local(): lax.all_to_all(blocked, ('pair', 'slab'), split_axis=0, concat_axis=0, ti...]
    transpose x2 -> x0, local copies, waits for them, and re-layouts: 7.27 us -> none  [local(): cycle_term.reshape(own_rows, pair_count, own_rows, tile_width, slab_count...]
    reshape x1 -> x0, local copies, waits for them, and re-layouts: 3.78 us -> none  [local(): mirrored = mirrored.reshape(own_rows, occ_count, tile_width, virt_count)]
  transfers between devices with their start and end apart: 2 -> 0, of which waited for: 2 -> 0; matrix products, arithmetic and copies ran while one was open for 3% -> 0% of each run, Pallas kernels for 0% -> 0%
where the time goes in v2:
time: 28 us; the launch traced here: 27.8 us
  Pallas kernels  26.5 us (95%)
  local copies, waits for them, and re-layouts  1.32 us (5%)
    pallas_call x1, Pallas kernels, local(): pl.pallas_call(kernel, out_shape=jax.ShapeDtypeStruct((1, NJ, TILE, V), F...  26.5 us
    unnamed x1, local copies, waits for them, and re-layouts  1.32 us

profile of v2, /device:TPU:0, one launch (start us, length us, event | category | flops | bytes accessed | tf_op | source)
XLA Modules:
  0.0 27.8 jit_solution(5107781094669345860)
XLA Ops:
  0.0 26.5 %shard_map.55 = f32[1,16,64,512]{3,2,1,0:T(8,128)S(1)} custom-call(bf16[4,2,64,512]{3,2,1,0:T(8,128)(2,1)} %bitcast.3, bf16[8,1,64,512]{3,2,1,0:T(8,128)(2,1)} %ints_hbm.1, s32[16]{0:T(128)} %bitcast.5, s32[8]{0:T(128)} %slab_hbm.1, s32[1,512]{1,0:T(1,128)} %bitcast.4), custom_call_target="tpu_custom_call" | custom-call | tf_op jit(solution)/shard_map/pallas_call | solution.py:221
  26.5 1.3 %copy.7 = f32[1,16,64,512]{3,2,1,0:T(8,128)} copy(f32[1,16,64,512]{3,2,1,0:T(8,128)S(1)} %shard_map.55) | data formatting | bytes 4194304

commit v3 on v2

v3 whole, which is shorter than its diff:
```python
import jax
import jax.numpy as jnp
from jax import lax
from jax.experimental import pallas as pl
from jax.experimental.pallas import tpu as pltpu
from jax.sharding import PartitionSpec as P

NX = NY = NZ = 4
NJ = 16
NS = 8
TILE = 64
V = 512
N_SEMS = 37
N_SENT = 204
STEPS = (1, -1, 2)
BF16 = jnp.bfloat16
F32 = jnp.float32


def wrap(at, step, size):
    return lax.rem(at + step + size, size)


def kernel(
    amps_hbm, ints_hbm, occ_hbm, slab_hbm, virt_hbm, out_ref,
    amps, ints, occ_ref, slab_ref, virt_ref, row_labels, from_sibling, part, from_ring,
    pair_w, pair_a, slab_w, slab_a, spent, load_sems, send_sems, recv_sems,
):
    pair, slab = lax.axis_index("pair"), lax.axis_index("slab")
    z, x = pair // NX, lax.rem(pair, NX)
    y, core = slab // 2, lax.rem(slab, 2)
    sibling_core = 1 - core

    def at_pair(dz, dx):
        return wrap(z, dz, NZ) * NX + wrap(x, dx, NX)

    def at_slab(dy, own_core=True):
        return wrap(y, dy, NY) * 2 + (core if own_core else sibling_core)

    device = {"sibling": (pair, at_slab(0, False))}
    for step in STEPS:
        device["x", step] = (at_pair(0, step), slab)
        device["z", step] = (at_pair(step, 0), slab)
        device["y", step] = (pair, at_slab(step))

    loads = [
        pltpu.make_async_copy(src, dst, load_sems.at[at])
        for at, (src, dst) in enumerate((
            (virt_hbm, virt_ref),
            (occ_hbm, occ_ref),
            (slab_hbm, slab_ref),
            (amps_hbm.at[:, core], amps),
            (ints_hbm.at[:, 0], ints),
        ))
    ]
    for load in loads:
        load.start()

    barrier = pltpu.get_barrier_semaphore()
    for to in device.values():
        pl.semaphore_signal(barrier, inc=1, device_id=to, device_id_type=pl.DeviceIdType.MESH)

    order, sent = {}, []

    def copy(group, src, dst, to):
        at = order.setdefault(group, len(order))
        return pltpu.make_async_remote_copy(
            src_ref=src, dst_ref=dst, send_sem=send_sems.at[0], recv_sem=recv_sems.at[at],
            device_id=device[to], device_id_type=pl.DeviceIdType.MESH,
        )

    def send(group, src, dst, to):
        copy(group, src, dst, to).start()
        sent.append(src.size // (16 * V))

    def arrive(group, like):
        copy(group, like, like, "sibling").wait_recv()

    pl.semaphore_wait(barrier, len(device))
    send("merge", amps_hbm.at[:, sibling_core], from_sibling, "sibling")

    for load in loads[:3]:
        load.wait()
    columns = virt_ref[...]
    for at in range(V // 128):
        lanes = jnp.broadcast_to(columns[:, at * 128 : (at + 1) * 128], (128, 128))
        row_labels[at * 128 : (at + 1) * 128, :] = lanes.T

    def pair_labels(tile):
        rows = row_labels[pl.ds(pl.multiple_of(tile * TILE, TILE), TILE), :]
        return jnp.concatenate([rows] * (V // 128), axis=1) ^ columns

    own_label = occ_ref[pair]
    amps_label = own_label ^ slab_ref[slab]
    sibling_label = own_label ^ slab_ref[at_slab(0, False)]

    loads[4].wait()
    wanted = pair_labels(slab) ^ own_label
    w = jnp.zeros((TILE, V), F32)
    for k in range(8):
        w = jnp.where(wanted == slab_ref[k], ints[k].astype(F32), w)
    w = w.astype(BF16).reshape(2, 2, 16, V)
    pair_w[pair] = w
    slab_w[slab] = w

    axes = (("x", "z", 0), ("z", "x", 1))

    def beside(axis, step, other=0):
        return at_pair(other, step) if axis == "x" else at_pair(step, other)

    def pair_start(tag, buf, chunk):
        for step in STEPS:
            for axis, _, half in axes:
                own = buf.at[pair, half, chunk]
                send((tag, str(chunk), axis, step), own, own, (axis, step))
        for step in STEPS:
            for axis, _, half in axes:
                own = buf.at[pair, 1 - half, chunk]
                send((tag, "own"), own, own, (axis, step))

    def pair_turn(tag, buf, chunk):
        for step in STEPS:
            for axis, other, half in axes:
                piece = buf.at[beside(axis, -step), half, chunk]
                arrive((tag, str(chunk), axis, step), piece)
                for way in STEPS:
                    send((tag, "turned", step if axis == "x" else way), piece, piece, (other, way))

    def pair_near(tag, buf):
        arrive((tag, "own"), buf.at[pl.ds(0, 3)])

    def pair_end(tag, buf, step):
        arrive((tag, "turned", step), buf.at[pl.ds(0, 3)])

    def slab_start(tag, buf):
        for step in STEPS:
            send((tag, step), buf.at[slab], buf.at[slab], ("y", step))
        send((tag, "sibling"), buf.at[slab], buf.at[slab], "sibling")

    def slab_over(tag, buf):
        for step in STEPS:
            piece = buf.at[at_slab(-step)]
            arrive((tag, step), piece)
            send((tag, "sibling"), piece, piece, "sibling")

    def slab_end(tag, buf):
        arrive((tag, "sibling"), buf.at[pl.ds(0, NY)])

    whole = pl.ds(0, 2)
    pair_start("pw", pair_w, whole)

    loads[3].wait()
    arrive("merge", from_sibling)
    for at in range(NY):
        labels = pair_labels(2 * at + core)
        other = jnp.where(labels == sibling_label, from_sibling[at].astype(F32), 0.0)
        part[at] = jnp.where(labels == amps_label, amps[at].astype(F32), other).astype(BF16).reshape(2, 2, 16, V)
    for chunk in range(2):
        for at, step in enumerate(STEPS):
            send(("ring", chunk), part.at[wrap(y, step, NY), :, chunk], from_ring.at[at, :, chunk], ("y", step))
    slab_start("sw", slab_w)

    def ring_end(chunk):
        arrive(("ring", chunk), from_ring.at[:, :, chunk])
        total = part[y, :, chunk]
        for at in range(len(STEPS)):
            total = total + from_ring[at, :, chunk]
        pair_a[pair, :, chunk] = total
        slab_a[slab, :, chunk] = total

    pair_turn("pw", pair_w, whole)
    for chunk in range(2):
        ring_end(chunk)
        pair_start("pa", pair_a, chunk)
    slab_start("sa", slab_a)
    slab_over("sw", slab_w)
    for chunk in range(2):
        pair_turn("pa", pair_a, chunk)
    slab_over("sa", slab_a)
    pair_near("pw", pair_w)
    for step in STEPS:
        pair_end("pw", pair_w, step)
    slab_end("sw", slab_w)
    slab_end("sa", slab_a)

    def times(rows, every):
        return lax.dot_general(rows, every, (((1,), (1,)), ((), ())), preferred_element_type=F32)

    @pl.loop(0, 2)
    def _(at):
        half = NJ // 2
        rows = pair_w[pl.ds(at * half, half)].reshape(half * TILE, V)
        out_ref[0, pl.ds(at * half, half)] = times(rows, slab_a[...].reshape(V, V)).reshape(half, TILE, V)

    labels = pair_labels(slab) ^ own_label

    def second_term(group):
        rows = jnp.concatenate([pair_a[j].reshape(TILE, V) for j in group], axis=0)
        term = times(rows, slab_w[...].reshape(V, V))
        for at, j in enumerate(group):
            both = out_ref[0, j] + term[at * TILE : (at + 1) * TILE]
            out_ref[0, j] = jnp.where(labels == occ_ref[j], both, 0.0)

    pair_near("pa", pair_a)
    second_term([pair] + [beside(axis, step) for axis in ("x", "z") for step in STEPS])
    for step in STEPS:
        pair_end("pa", pair_a, step)
        second_term([beside("x", -step, -way) for way in STEPS])

    assert len(order) == N_SEMS
    assert sum(sent) == N_SENT
    copy("merge", spent, spent, "sibling").wait_send()


def solution(mesh):
    placed = (P("pair", "slab", None, None), P(None, "pair", "slab", None), P(), P(), P())
    piece = (2, 2, 16, V)

    def local(amplitudes, integrals, occ_irrep, slab_irrep, virt_irrep):
        operands = (
            amplitudes.reshape(NY, 2, TILE, V), integrals, occ_irrep.reshape(NJ), slab_irrep, virt_irrep.reshape(1, V)
        )
        return pl.pallas_call(
            kernel,
            out_shape=jax.ShapeDtypeStruct((1, NJ, TILE, V), F32),
            in_specs=[pl.BlockSpec(memory_space=pltpu.HBM)] * 5,
            out_specs=pl.BlockSpec(memory_space=pltpu.VMEM),
            scratch_shapes=[
                pltpu.VMEM((NY, TILE, V), BF16),
                pltpu.VMEM((8, TILE, V), BF16),
                pltpu.SMEM((NJ,), jnp.int32),
                pltpu.SMEM((8,), jnp.int32),
                pltpu.VMEM((1, V), jnp.int32),
                pltpu.VMEM((V, 128), jnp.int32),
                pltpu.VMEM((NY, TILE, V), BF16),
                pltpu.VMEM((NY, *piece), BF16),
                pltpu.VMEM((3, *piece), BF16),
                pltpu.VMEM((NJ, *piece), BF16),
                pltpu.VMEM((NJ, *piece), BF16),
                pltpu.VMEM((NS, *piece), BF16),
                pltpu.VMEM((NS, *piece), BF16),
                pltpu.VMEM((N_SENT, 16, V), BF16),
                pltpu.SemaphoreType.DMA((5,)),
                pltpu.SemaphoreType.DMA((1,)),
                pltpu.SemaphoreType.DMA((N_SEMS,)),
            ],
            compiler_params=pltpu.CompilerParams(
                collective_id=0, has_side_effects=True, vmem_limit_bytes=32 * 1024 * 1024
            ),
        )(*(pltpu.with_memory_space_constraint(operand, pltpu.HBM) for operand in operands))

    return jax.shard_map(
        local, mesh=mesh, in_specs=placed, out_specs=P("pair", None, "slab", None), check_vma=False
    )
```

time: 28 us -> 26.4 us (0.943)
  Pallas kernels: 26.5 us -> 25 us
    pallas_call x1, Pallas kernels: 26.5 us -> 25 us  [local(): pl.pallas_call(kernel, out_shape=jax.ShapeDtypeStruct((1, NJ, TILE, V), F...]
where the time goes in v3:
time: 26.4 us; the launch traced here: 26.3 us
  Pallas kernels  25 us (95%)
  local copies, waits for them, and re-layouts  1.32 us (5%)
    pallas_call x1, Pallas kernels, local(): pl.pallas_call(kernel, out_shape=jax.ShapeDtypeStruct((1, NJ, TILE, V), F...  25 us
    unnamed x1, local copies, waits for them, and re-layouts  1.32 us

profile of v3, /device:TPU:0, one launch (start us, length us, event | category | flops | bytes accessed | tf_op | source)
XLA Modules:
  0.0 26.3 jit_solution(2597532027165301689)
XLA Ops:
  0.0 25.0 %shard_map.55 = f32[1,16,64,512]{3,2,1,0:T(8,128)S(1)} custom-call(bf16[4,2,64,512]{3,2,1,0:T(8,128)(2,1)} %bitcast.3, bf16[8,1,64,512]{3,2,1,0:T(8,128)(2,1)} %ints_hbm.1, s32[16]{0:T(128)} %bitcast.5, s32[8]{0:T(128)} %slab_hbm.1, s32[1,512]{1,0:T(1,128)} %bitcast.4), custom_call_target="tpu_custom_call" | custom-call | tf_op jit(solution)/shard_map/pallas_call | solution.py:223
  25.0 1.3 %copy.7 = f32[1,16,64,512]{3,2,1,0:T(8,128)} copy(f32[1,16,64,512]{3,2,1,0:T(8,128)S(1)} %shard_map.55) | data formatting | bytes 4194304

commit v4 on v3

--- a/solution.py
+++ b/solution.py
@@ -10,8 +10,9 @@
 NS = 8
 TILE = 64
 V = 512
-N_SEMS = 37
+N_SEMS = 35
 N_SENT = 204
+NEAR = (1, -1)
 STEPS = (1, -1, 2)
 BF16 = jnp.bfloat16
 F32 = jnp.float32
@@ -109,35 +110,48 @@
         return at_pair(other, step) if axis == "x" else at_pair(step, other)
 
     def pair_start(tag, buf, chunk):
-        for step in STEPS:
+        for axis, _, _ in axes:
+            own = buf.at[pair, :, chunk]
+            send((tag, str(chunk), axis, 2), own, own, (axis, 2))
+        for step in NEAR:
             for axis, _, half in axes:
                 own = buf.at[pair, half, chunk]
                 send((tag, str(chunk), axis, step), own, own, (axis, step))
-        for step in STEPS:
+        for step in NEAR:
             for axis, _, half in axes:
                 own = buf.at[pair, 1 - half, chunk]
                 send((tag, "own"), own, own, (axis, step))
 
     def pair_turn(tag, buf, chunk):
-        for step in STEPS:
+        for step in NEAR:
             for axis, other, half in axes:
                 piece = buf.at[beside(axis, -step), half, chunk]
                 arrive((tag, str(chunk), axis, step), piece)
-                for way in STEPS:
-                    send((tag, "turned", step if axis == "x" else way), piece, piece, (other, way))
+                for way in NEAR:
+                    send((tag, "near"), piece, piece, (other, way))
+        for axis, other, half in axes:
+            piece = buf.at[beside(axis, 2), :, chunk]
+            arrive((tag, str(chunk), axis, 2), piece)
+            for way in NEAR:
+                send((tag, "far"), piece, piece, (other, way))
+            piece = buf.at[beside(axis, 2), half, chunk]
+            send((tag, "far"), piece, piece, (other, 2))
+
+    def pair_own(tag, buf):
+        arrive((tag, "own"), buf.at[pl.ds(0, 2)])
 
     def pair_near(tag, buf):
-        arrive((tag, "own"), buf.at[pl.ds(0, 3)])
-
-    def pair_end(tag, buf, step):
-        arrive((tag, "turned", step), buf.at[pl.ds(0, 3)])
-
-    def slab_start(tag, buf):
-        for step in STEPS:
+        arrive((tag, "near"), buf.at[pl.ds(0, 4)])
+
+    def pair_far(tag, buf):
+        arrive((tag, "far"), buf.at[pl.ds(0, 5)])
+
+    def slab_start(tag, buf, steps):
+        for step in steps:
             send((tag, step), buf.at[slab], buf.at[slab], ("y", step))
+
+    def slab_over(tag, buf):
         send((tag, "sibling"), buf.at[slab], buf.at[slab], "sibling")
-
-    def slab_over(tag, buf):
         for step in STEPS:
             piece = buf.at[at_slab(-step)]
             arrive((tag, step), piece)
@@ -148,6 +162,7 @@
 
     whole = pl.ds(0, 2)
     pair_start("pw", pair_w, whole)
+    slab_start("sw", slab_w, NEAR)
 
     loads[3].wait()
     arrive("merge", from_sibling)
@@ -158,7 +173,7 @@
     for chunk in range(2):
         for at, step in enumerate(STEPS):
             send(("ring", chunk), part.at[wrap(y, step, NY), :, chunk], from_ring.at[at, :, chunk], ("y", step))
-    slab_start("sw", slab_w)
+    slab_start("sw", slab_w, (2,))
 
     def ring_end(chunk):
         arrive(("ring", chunk), from_ring.at[:, :, chunk])
@@ -172,14 +187,14 @@
     for chunk in range(2):
         ring_end(chunk)
         pair_start("pa", pair_a, chunk)
-    slab_start("sa", slab_a)
+    slab_start("sa", slab_a, STEPS)
+    pair_turn("pa", pair_a, 0)
     slab_over("sw", slab_w)
-    for chunk in range(2):
-        pair_turn("pa", pair_a, chunk)
+    pair_turn("pa", pair_a, 1)
     slab_over("sa", slab_a)
+    pair_own("pw", pair_w)
     pair_near("pw", pair_w)
-    for step in STEPS:
-        pair_end("pw", pair_w, step)
+    pair_far("pw", pair_w)
     slab_end("sw", slab_w)
     slab_end("sa", slab_a)
 
@@ -201,11 +216,12 @@
             both = out_ref[0, j] + term[at * TILE : (at + 1) * TILE]
             out_ref[0, j] = jnp.where(labels == occ_ref[j], both, 0.0)
 
+    pair_own("pa", pair_a)
+    second_term([pair] + [beside(axis, step) for axis in ("x", "z") for step in STEPS])
     pair_near("pa", pair_a)
-    second_term([pair] + [beside(axis, step) for axis in ("x", "z") for step in STEPS])
-    for step in STEPS:
-        pair_end("pa", pair_a, step)
-        second_term([beside("x", -step, -way) for way in STEPS])
+    second_term([beside("x", step, way) for step in NEAR for way in NEAR])
+    pair_far("pa", pair_a)
+    second_term([beside(axis, 2, way) for axis in ("x", "z") for way in NEAR] + [beside("x", 2, 2)])
 
     assert len(order) == N_SEMS
     assert sum(sent) == N_SENT

time: 26.4 us -> 26.3 us (level)
  the two profiles are of different devices: /device:TPU:0 before, /device:TPU:1 now
where the time goes in v4:
time: 26.3 us; the launch traced here: 26.2 us
  Pallas kernels  24.8 us (94%)
  local copies, waits for them, and re-layouts  1.32 us (5%)
    pallas_call x1, Pallas kernels, local(): pl.pallas_call(kernel, out_shape=jax.ShapeDtypeStruct((1, NJ, TILE, V), F...  24.8 us
    unnamed x1, local copies, waits for them, and re-layouts  1.32 us

profile of v4, /device:TPU:1, one launch (start us, length us, event | category | flops | bytes accessed | tf_op | source)
XLA Modules:
  0.0 26.2 jit_solution(15841710484415287184)
XLA Ops:
  0.0 24.8 %shard_map.55 = f32[1,16,64,512]{3,2,1,0:T(8,128)S(1)} custom-call(bf16[4,2,64,512]{3,2,1,0:T(8,128)(2,1)} %bitcast.3, bf16[8,1,64,512]{3,2,1,0:T(8,128)(2,1)} %ints_hbm.1, s32[16]{0:T(128)} %bitcast.5, s32[8]{0:T(128)} %slab_hbm.1, s32[1,512]{1,0:T(1,128)} %bitcast.4), custom_call_target="tpu_custom_call" | custom-call | tf_op jit(solution)/shard_map/pallas_call | solution.py:239
  24.8 1.3 %copy.7 = f32[1,16,64,512]{3,2,1,0:T(8,128)} copy(f32[1,16,64,512]{3,2,1,0:T(8,128)S(1)} %shard_map.55) | data formatting | bytes 4194304

commit v5 on v4

--- a/solution.py
+++ b/solution.py
@@ -10,7 +10,7 @@
 NS = 8
 TILE = 64
 V = 512
-N_SEMS = 35
+N_SEMS = 25
 N_SENT = 204
 NEAR = (1, -1)
 STEPS = (1, -1, 2)
@@ -39,7 +39,7 @@
         return wrap(y, dy, NY) * 2 + (core if own_core else sibling_core)
 
     device = {"sibling": (pair, at_slab(0, False))}
-    for step in STEPS:
+    for step in (2, 1, -1):
         device["x", step] = (at_pair(0, step), slab)
         device["z", step] = (at_pair(step, 0), slab)
         device["y", step] = (pair, at_slab(step))
@@ -54,12 +54,13 @@
             (ints_hbm.at[:, 0], ints),
         ))
     ]
-    for load in loads:
-        load.start()
 
     barrier = pltpu.get_barrier_semaphore()
     for to in device.values():
         pl.semaphore_signal(barrier, inc=1, device_id=to, device_id_type=pl.DeviceIdType.MESH)
+
+    for load in loads:
+        load.start()
 
     order, sent = {}, []
 
@@ -109,29 +110,34 @@
     def beside(axis, step, other=0):
         return at_pair(other, step) if axis == "x" else at_pair(step, other)
 
-    def pair_start(tag, buf, chunk):
+    def start_far(tag, buf, chunk):
         for axis, _, _ in axes:
             own = buf.at[pair, :, chunk]
-            send((tag, str(chunk), axis, 2), own, own, (axis, 2))
+            send((tag, str(chunk), 2), own, own, (axis, 2))
+
+    def start_near(tag, buf, chunk):
         for step in NEAR:
             for axis, _, half in axes:
                 own = buf.at[pair, half, chunk]
-                send((tag, str(chunk), axis, step), own, own, (axis, step))
+                send((tag, str(chunk), 1), own, own, (axis, step))
+
+    def start_own(tag, buf, chunk):
         for step in NEAR:
             for axis, _, half in axes:
                 own = buf.at[pair, 1 - half, chunk]
                 send((tag, "own"), own, own, (axis, step))
 
-    def pair_turn(tag, buf, chunk):
+    def turn_near(tag, buf, chunk):
+        arrive((tag, str(chunk), 1), buf.at[pl.ds(0, 2), :, chunk])
         for step in NEAR:
             for axis, other, half in axes:
                 piece = buf.at[beside(axis, -step), half, chunk]
-                arrive((tag, str(chunk), axis, step), piece)
                 for way in NEAR:
                     send((tag, "near"), piece, piece, (other, way))
+    def turn_far(tag, buf, chunk):
+        arrive((tag, str(chunk), 2), buf.at[pl.ds(0, 2), :, chunk])
         for axis, other, half in axes:
             piece = buf.at[beside(axis, 2), :, chunk]
-            arrive((tag, str(chunk), axis, 2), piece)
             for way in NEAR:
                 send((tag, "far"), piece, piece, (other, way))
             piece = buf.at[beside(axis, 2), half, chunk]
@@ -161,7 +167,11 @@
         arrive((tag, "sibling"), buf.at[pl.ds(0, NY)])
 
     whole = pl.ds(0, 2)
-    pair_start("pw", pair_w, whole)
+    start_far("pw", pair_w, 0)
+    start_near("pw", pair_w, 0)
+    start_far("pw", pair_w, 1)
+    start_near("pw", pair_w, 1)
+    start_own("pw", pair_w, whole)
     slab_start("sw", slab_w, NEAR)
 
     loads[3].wait()
@@ -183,14 +193,25 @@
         pair_a[pair, :, chunk] = total
         slab_a[slab, :, chunk] = total
 
-    pair_turn("pw", pair_w, whole)
-    for chunk in range(2):
-        ring_end(chunk)
-        pair_start("pa", pair_a, chunk)
+    turn_near("pw", pair_w, 0)
+    turn_far("pw", pair_w, 0)
+    turn_near("pw", pair_w, 1)
+    turn_far("pw", pair_w, 1)
+    ring_end(0)
+    start_far("pa", pair_a, 0)
+    start_near("pa", pair_a, 0)
+    ring_end(1)
+    start_far("pa", pair_a, 1)
+    start_near("pa", pair_a, 1)
+    start_own("pa", pair_a, 0)
+    start_own("pa", pair_a, 1)
     slab_start("sa", slab_a, STEPS)
-    pair_turn("pa", pair_a, 0)
+    turn_far("pa", pair_a, 0)
+    turn_near("pa", pair_a, 0)
     slab_over("sw", slab_w)
-    pair_turn("pa", pair_a, 1)
+    turn_far("pa", pair_a, 1)
+    turn_near("pa", pair_a, 1)
+
     slab_over("sa", slab_a)
     pair_own("pw", pair_w)
     pair_near("pw", pair_w)
@@ -223,7 +244,6 @@
     pair_far("pa", pair_a)
     second_term([beside(axis, 2, way) for axis in ("x", "z") for way in NEAR] + [beside("x", 2, 2)])
 
-    assert len(order) == N_SEMS
     assert sum(sent) == N_SENT
     copy("merge", spent, spent, "sibling").wait_send()
 

time: 26.3 us -> 24.9 us (0.947)
  the two profiles are of different devices: /device:TPU:1 before, /device:TPU:0 now
where the time goes in v5:
time: 24.9 us; the launch traced here: 24.8 us
  Pallas kernels  23.4 us (94%)
  local copies, waits for them, and re-layouts  1.32 us (5%)
    pallas_call x1, Pallas kernels, local(): pl.pallas_call(kernel, out_shape=jax.ShapeDtypeStruct((1, NJ, TILE, V), F...  23.4 us
    unnamed x1, local copies, waits for them, and re-layouts  1.32 us

profile of v5, /device:TPU:0, one launch (start us, length us, event | category | flops | bytes accessed | tf_op | source)
XLA Modules:
  0.0 24.8 jit_solution(6876305550983350786)
XLA Ops:
  0.0 23.4 %shard_map.55 = f32[1,16,64,512]{3,2,1,0:T(8,128)S(1)} custom-call(bf16[4,2,64,512]{3,2,1,0:T(8,128)(2,1)} %bitcast.3, bf16[8,1,64,512]{3,2,1,0:T(8,128)(2,1)} %ints_hbm.1, s32[16]{0:T(128)} %bitcast.5, s32[8]{0:T(128)} %slab_hbm.1, s32[1,512]{1,0:T(1,128)} %bitcast.4), custom_call_target="tpu_custom_call" | custom-call | tf_op jit(solution)/shard_map/pallas_call | solution.py:259
  23.4 1.3 %copy.7 = f32[1,16,64,512]{3,2,1,0:T(8,128)} copy(f32[1,16,64,512]{3,2,1,0:T(8,128)S(1)} %shard_map.55) | data formatting | bytes 4194304

commit v6 on v5

--- a/solution.py
+++ b/solution.py
@@ -10,7 +10,7 @@
 NS = 8
 TILE = 64
 V = 512
-N_SEMS = 25
+N_SEMS = 26
 N_SENT = 204
 NEAR = (1, -1)
 STEPS = (1, -1, 2)
@@ -22,8 +22,40 @@
     return lax.rem(at + step + size, size)
 
 
+def times(rows, every):
+    return lax.dot_general(rows, every, (((1,), (1,)), ((), ())), preferred_element_type=F32)
+
+
+def pieces_at(z, x, steps):
+    return [wrap(z, dz, NZ) * NX + wrap(x, dx, NX) for dz, dx in steps]
+
+
+def near_pieces(z, x):
+    return pieces_at(z, x, [(0, 0)] + [(0, s) for s in STEPS] + [(s, 0) for s in STEPS] + [(a, b) for a in NEAR for b in NEAR])
+
+
+def far_pieces(z, x):
+    return pieces_at(z, x, [(2, s) for s in STEPS] + [(s, 2) for s in NEAR])
+
+
+def finish(done_ref, rows_ref, every_ref, labels_ref, late_ref, out_hbm, last, sems):
+    pair = lax.axis_index("pair")
+    z, x = pair // NX, lax.rem(pair, NX)
+    near, far = near_pieces(z, x), far_pieces(z, x)
+    for j in near:
+        pltpu.make_async_copy(done_ref.at[j], out_hbm.at[j], sems.at[0]).start()
+    term = times(rows_ref[...], every_ref[...])
+    for at, j in enumerate(far):
+        kept = labels_ref[...] == jnp.concatenate([late_ref[at : at + 1, :]] * (V // 128), axis=1)
+        last[at] = jnp.where(kept, done_ref[j] + term[at * TILE : (at + 1) * TILE], 0.0)
+        pltpu.make_async_copy(last.at[at], out_hbm.at[j], sems.at[1]).start()
+    many = done_ref.at[pl.ds(0, len(near))]
+    pltpu.make_async_copy(many, out_hbm.at[pl.ds(0, len(near))], sems.at[0]).wait()
+    pltpu.make_async_copy(last, out_hbm.at[pl.ds(0, len(far))], sems.at[1]).wait()
+
+
 def kernel(
-    amps_hbm, ints_hbm, occ_hbm, slab_hbm, virt_hbm, out_ref,
+    amps_hbm, ints_hbm, occ_hbm, slab_hbm, virt_hbm, out_ref, rows_ref, every_ref, labels_ref, late_ref,
     amps, ints, occ_ref, slab_ref, virt_ref, row_labels, from_sibling, part, from_ring,
     pair_w, pair_a, slab_w, slab_a, spent, load_sems, send_sems, recv_sems,
 ):
@@ -79,7 +111,8 @@
         copy(group, like, like, "sibling").wait_recv()
 
     pl.semaphore_wait(barrier, len(device))
-    send("merge", amps_hbm.at[:, sibling_core], from_sibling, "sibling")
+    for chunk in range(2):
+        send(("merge", chunk), amps_hbm.at[:, sibling_core, :, chunk], from_sibling.at[:, :, chunk], "sibling")
 
     for load in loads[:3]:
         load.wait()
@@ -175,19 +208,21 @@
     slab_start("sw", slab_w, NEAR)
 
     loads[3].wait()
-    arrive("merge", from_sibling)
-    for at in range(NY):
-        labels = pair_labels(2 * at + core)
-        other = jnp.where(labels == sibling_label, from_sibling[at].astype(F32), 0.0)
-        part[at] = jnp.where(labels == amps_label, amps[at].astype(F32), other).astype(BF16).reshape(2, 2, 16, V)
+    def merged(at, chunk):
+        labels = pair_labels(2 * at + core).reshape(2, 2, 16, V)[:, chunk]
+        other = jnp.where(labels == sibling_label, from_sibling[at, :, chunk].astype(F32), 0.0)
+        return jnp.where(labels == amps_label, amps[at, :, chunk].astype(F32), other).astype(BF16)
+
     for chunk in range(2):
+        arrive(("merge", chunk), from_sibling.at[:, :, chunk])
         for at, step in enumerate(STEPS):
-            send(("ring", chunk), part.at[wrap(y, step, NY), :, chunk], from_ring.at[at, :, chunk], ("y", step))
+            part[at, :, chunk] = merged(wrap(y, step, NY), chunk)
+            send(("ring", chunk), part.at[at, :, chunk], from_ring.at[at, :, chunk], ("y", step))
     slab_start("sw", slab_w, (2,))
 
     def ring_end(chunk):
+        total = merged(y, chunk)
         arrive(("ring", chunk), from_ring.at[:, :, chunk])
-        total = part[y, :, chunk]
         for at in range(len(STEPS)):
             total = total + from_ring[at, :, chunk]
         pair_a[pair, :, chunk] = total
@@ -219,14 +254,11 @@
     slab_end("sw", slab_w)
     slab_end("sa", slab_a)
 
-    def times(rows, every):
-        return lax.dot_general(rows, every, (((1,), (1,)), ((), ())), preferred_element_type=F32)
-
     @pl.loop(0, 2)
     def _(at):
         half = NJ // 2
         rows = pair_w[pl.ds(at * half, half)].reshape(half * TILE, V)
-        out_ref[0, pl.ds(at * half, half)] = times(rows, slab_a[...].reshape(V, V)).reshape(half, TILE, V)
+        out_ref[pl.ds(at * half, half)] = times(rows, slab_a[...].reshape(V, V)).reshape(half, TILE, V)
 
     labels = pair_labels(slab) ^ own_label
 
@@ -234,18 +266,23 @@
         rows = jnp.concatenate([pair_a[j].reshape(TILE, V) for j in group], axis=0)
         term = times(rows, slab_w[...].reshape(V, V))
         for at, j in enumerate(group):
-            both = out_ref[0, j] + term[at * TILE : (at + 1) * TILE]
-            out_ref[0, j] = jnp.where(labels == occ_ref[j], both, 0.0)
+            both = out_ref[j] + term[at * TILE : (at + 1) * TILE]
+            out_ref[j] = jnp.where(labels == occ_ref[j], both, 0.0)
 
     pair_own("pa", pair_a)
     second_term([pair] + [beside(axis, step) for axis in ("x", "z") for step in STEPS])
     pair_near("pa", pair_a)
     second_term([beside("x", step, way) for step in NEAR for way in NEAR])
+    every_ref[...] = slab_w[...].reshape(V, V)
+    labels_ref[...] = labels
+    for at, j in enumerate(far_pieces(z, x)):
+        late_ref[at : at + 1, :] = jnp.full((1, 128), occ_ref[j], jnp.int32)
     pair_far("pa", pair_a)
-    second_term([beside(axis, 2, way) for axis in ("x", "z") for way in NEAR] + [beside("x", 2, 2)])
+    for at, j in enumerate(far_pieces(z, x)):
+        rows_ref[at * TILE : (at + 1) * TILE, :] = pair_a[j].reshape(TILE, V)
 
     assert sum(sent) == N_SENT
-    copy("merge", spent, spent, "sibling").wait_send()
+    copy(("merge", 0), spent, spent, "sibling").wait_send()
 
 
 def solution(mesh):
@@ -254,22 +291,28 @@
 
     def local(amplitudes, integrals, occ_irrep, slab_irrep, virt_irrep):
         operands = (
-            amplitudes.reshape(NY, 2, TILE, V), integrals, occ_irrep.reshape(NJ), slab_irrep, virt_irrep.reshape(1, V)
+            amplitudes.reshape(NY, 2, *piece), integrals, occ_irrep.reshape(NJ), slab_irrep, virt_irrep.reshape(1, V)
         )
-        return pl.pallas_call(
+        gathered = pl.pallas_call(
             kernel,
-            out_shape=jax.ShapeDtypeStruct((1, NJ, TILE, V), F32),
+            out_shape=(
+                jax.ShapeDtypeStruct((NJ, TILE, V), F32),
+                jax.ShapeDtypeStruct((5 * TILE, V), BF16),
+                jax.ShapeDtypeStruct((V, V), BF16),
+                jax.ShapeDtypeStruct((TILE, V), jnp.int32),
+                jax.ShapeDtypeStruct((8, 128), jnp.int32),
+            ),
             in_specs=[pl.BlockSpec(memory_space=pltpu.HBM)] * 5,
-            out_specs=pl.BlockSpec(memory_space=pltpu.VMEM),
+            out_specs=[pl.BlockSpec(memory_space=pltpu.VMEM)] * 5,
             scratch_shapes=[
-                pltpu.VMEM((NY, TILE, V), BF16),
+                pltpu.VMEM((NY, *piece), BF16),
                 pltpu.VMEM((8, TILE, V), BF16),
                 pltpu.SMEM((NJ,), jnp.int32),
                 pltpu.SMEM((8,), jnp.int32),
                 pltpu.VMEM((1, V), jnp.int32),
                 pltpu.VMEM((V, 128), jnp.int32),
-                pltpu.VMEM((NY, TILE, V), BF16),
                 pltpu.VMEM((NY, *piece), BF16),
+                pltpu.VMEM((3, *piece), BF16),
                 pltpu.VMEM((3, *piece), BF16),
                 pltpu.VMEM((NJ, *piece), BF16),
                 pltpu.VMEM((NJ, *piece), BF16),
@@ -284,6 +327,15 @@
                 collective_id=0, has_side_effects=True, vmem_limit_bytes=32 * 1024 * 1024
             ),
         )(*(pltpu.with_memory_space_constraint(operand, pltpu.HBM) for operand in operands))
+        residual = pl.pallas_call(
+            finish,
+            out_shape=jax.ShapeDtypeStruct((NJ, TILE, V), F32),
+            in_specs=[pl.BlockSpec(memory_space=pltpu.VMEM)] * 5,
+            out_specs=pl.BlockSpec(memory_space=pltpu.HBM),
+            scratch_shapes=[pltpu.VMEM((5, TILE, V), F32), pltpu.SemaphoreType.DMA((2,))],
+            compiler_params=pltpu.CompilerParams(vmem_limit_bytes=16 * 1024 * 1024),
+        )(*gathered)
+        return residual[None]
 
     return jax.shard_map(
         local, mesh=mesh, in_specs=placed, out_specs=P("pair", None, "slab", None), check_vma=False

time: 24.9 us -> 24.5 us (0.984)
  local copies, waits for them, and re-layouts: 1.32 us -> 0 us
  Pallas kernels: 23.4 us -> 24.3 us
    unnamed x1 -> x0, local copies, waits for them, and re-layouts: 1.32 us -> none
    pallas_call x1 -> x2, Pallas kernels: 23.4 us -> 24.3 us  [the longest x1 22.9 us: local(): pl.pallas_call(kernel, out_shape=(jax.ShapeDtypeStruct((NJ, TILE, V), F32...]
where the time goes in v6:
time: 24.5 us; the launch traced here: 24.3 us
  Pallas kernels  24.3 us (99%)
    pallas_call x1, Pallas kernels, local(): pl.pallas_call(kernel, out_shape=(jax.ShapeDtypeStruct((NJ, TILE, V), F32...  22.9 us
    pallas_call x1, Pallas kernels, local(): pl.pallas_call(finish, out_shape=jax.ShapeDtypeStruct((NJ, TILE, V), F32)...  1.42 us

profile of v6, /device:TPU:0, one launch (start us, length us, event | category | flops | bytes accessed | tf_op | source)
XLA Modules:
  0.0 24.3 jit_solution(3118046340533112686)
XLA Ops:
  0.0 22.9 %shard_map.55 = (f32[16,64,512]{2,1,0:T(8,128)S(1)}, bf16[320,512]{1,0:T(8,128)(2,1)S(1)}, bf16[512,512]{1,0:T(8,128)(2,1)S(1)}, s32[64,512]{1,0:T(8,128)S(1)}, s32[8,128]{1,0:T(8,128)S(1)}) custom-call(bf16[4,2,2,2,16,512]{5,4,3,2,1,0:T(8,128)(2,1)} %bitcast.4, bf16[8,1,64,512]{3,2,1,0:T(8,128)(2,1)} %ints_hbm.1, s32[16]{0:T(128)} %bitcast.6, s32[8]{0:T(128)} %slab_hbm.1, ...), custom_call_target="tpu_custom_call" | custom-call | tf_op jit(solution)/shard_map/pallas_call | solution.py:296
  22.9 1.4 %shard_map.56 = f32[16,64,512]{2,1,0:T(8,128)} custom-call(f32[16,64,512]{2,1,0:T(8,128)S(1)} %get-tuple-element.10.done_ref, bf16[320,512]{1,0:T(8,128)(2,1)S(1)} %get-tuple-element.11.rows_ref, bf16[512,512]{1,0:T(8,128)(2,1)S(1)} %get-tuple-element.12.every_ref, s32[64,512]{1,0:T(8,128)S(1)} %get-tuple-element.13.labels_ref, ...), custom_call_target="tpu_custom_call" | custom-call | tf_op jit(solution)/shard_map/pallas_call | solution.py:330

commit v7 on v6

--- a/solution.py
+++ b/solution.py
@@ -31,11 +31,11 @@
 
 
 def near_pieces(z, x):
-    return pieces_at(z, x, [(0, 0)] + [(0, s) for s in STEPS] + [(s, 0) for s in STEPS] + [(a, b) for a in NEAR for b in NEAR])
+    return pieces_at(z, x, [(0, 0)] + [(0, s) for s in STEPS] + [(s, 0) for s in STEPS])
 
 
 def far_pieces(z, x):
-    return pieces_at(z, x, [(2, s) for s in STEPS] + [(s, 2) for s in NEAR])
+    return pieces_at(z, x, [(a, b) for a in NEAR for b in NEAR] + [(2, s) for s in STEPS] + [(s, 2) for s in NEAR])
 
 
 def finish(done_ref, rows_ref, every_ref, labels_ref, late_ref, out_hbm, last, sems):
@@ -44,11 +44,13 @@
     near, far = near_pieces(z, x), far_pieces(z, x)
     for j in near:
         pltpu.make_async_copy(done_ref.at[j], out_hbm.at[j], sems.at[0]).start()
-    term = times(rows_ref[...], every_ref[...])
-    for at, j in enumerate(far):
-        kept = labels_ref[...] == jnp.concatenate([late_ref[at : at + 1, :]] * (V // 128), axis=1)
-        last[at] = jnp.where(kept, done_ref[j] + term[at * TILE : (at + 1) * TILE], 0.0)
-        pltpu.make_async_copy(last.at[at], out_hbm.at[j], sems.at[1]).start()
+    for first, after in ((0, 4), (4, 9)):
+        term = times(rows_ref[first * TILE : after * TILE, :], every_ref[...])
+        for at in range(first, after):
+            kept = labels_ref[...] == jnp.concatenate([late_ref[at : at + 1, :]] * (V // 128), axis=1)
+            both = done_ref[far[at]] + term[(at - first) * TILE : (at - first + 1) * TILE]
+            last[at] = jnp.where(kept, both, 0.0)
+            pltpu.make_async_copy(last.at[at], out_hbm.at[far[at]], sems.at[1]).start()
     many = done_ref.at[pl.ds(0, len(near))]
     pltpu.make_async_copy(many, out_hbm.at[pl.ds(0, len(near))], sems.at[0]).wait()
     pltpu.make_async_copy(last, out_hbm.at[pl.ds(0, len(far))], sems.at[1]).wait()
@@ -271,14 +273,14 @@
 
     pair_own("pa", pair_a)
     second_term([pair] + [beside(axis, step) for axis in ("x", "z") for step in STEPS])
-    pair_near("pa", pair_a)
-    second_term([beside("x", step, way) for step in NEAR for way in NEAR])
     every_ref[...] = slab_w[...].reshape(V, V)
     labels_ref[...] = labels
     for at, j in enumerate(far_pieces(z, x)):
         late_ref[at : at + 1, :] = jnp.full((1, 128), occ_ref[j], jnp.int32)
-    pair_far("pa", pair_a)
+    pair_near("pa", pair_a)
     for at, j in enumerate(far_pieces(z, x)):
+        if at == 4:
+            pair_far("pa", pair_a)
         rows_ref[at * TILE : (at + 1) * TILE, :] = pair_a[j].reshape(TILE, V)
 
     assert sum(sent) == N_SENT
@@ -297,10 +299,10 @@
             kernel,
             out_shape=(
                 jax.ShapeDtypeStruct((NJ, TILE, V), F32),
-                jax.ShapeDtypeStruct((5 * TILE, V), BF16),
+                jax.ShapeDtypeStruct((9 * TILE, V), BF16),
                 jax.ShapeDtypeStruct((V, V), BF16),
                 jax.ShapeDtypeStruct((TILE, V), jnp.int32),
-                jax.ShapeDtypeStruct((8, 128), jnp.int32),
+                jax.ShapeDtypeStruct((16, 128), jnp.int32),
             ),
             in_specs=[pl.BlockSpec(memory_space=pltpu.HBM)] * 5,
             out_specs=[pl.BlockSpec(memory_space=pltpu.VMEM)] * 5,
@@ -332,7 +334,7 @@
             out_shape=jax.ShapeDtypeStruct((NJ, TILE, V), F32),
             in_specs=[pl.BlockSpec(memory_space=pltpu.VMEM)] * 5,
             out_specs=pl.BlockSpec(memory_space=pltpu.HBM),
-            scratch_shapes=[pltpu.VMEM((5, TILE, V), F32), pltpu.SemaphoreType.DMA((2,))],
+            scratch_shapes=[pltpu.VMEM((9, TILE, V), F32), pltpu.SemaphoreType.DMA((2,))],
             compiler_params=pltpu.CompilerParams(vmem_limit_bytes=16 * 1024 * 1024),
         )(*gathered)
         return residual[None]

time: 24.5 us -> 24.1 us (0.984)
  Pallas kernels: 24.3 us -> 23.9 us
    pallas_call x1, Pallas kernels: 22.9 us -> 22.5 us  [local(): pl.pallas_call(kernel, out_shape=(jax.ShapeDtypeStruct((NJ, TILE, V), F32...]
where the time goes in v7:
time: 24.1 us; the launch traced here: 23.9 us
  Pallas kernels  23.9 us (99%)
    pallas_call x1, Pallas kernels, local(): pl.pallas_call(kernel, out_shape=(jax.ShapeDtypeStruct((NJ, TILE, V), F32...  22.5 us
    pallas_call x1, Pallas kernels, local(): pl.pallas_call(finish, out_shape=jax.ShapeDtypeStruct((NJ, TILE, V), F32)...  1.34 us

profile of v7, /device:TPU:0, one launch (start us, length us, event | category | flops | bytes accessed | tf_op | source)
XLA Modules:
  0.0 23.9 jit_solution(11709252782558238426)
XLA Ops:
  0.0 22.5 %shard_map.55 = (f32[16,64,512]{2,1,0:T(8,128)S(1)}, bf16[576,512]{1,0:T(8,128)(2,1)S(1)}, bf16[512,512]{1,0:T(8,128)(2,1)S(1)}, s32[64,512]{1,0:T(8,128)S(1)}, s32[16,128]{1,0:T(8,128)S(1)}) custom-call(bf16[4,2,2,2,16,512]{5,4,3,2,1,0:T(8,128)(2,1)} %bitcast.4, bf16[8,1,64,512]{3,2,1,0:T(8,128)(2,1)} %ints_hbm.1, s32[16]{0:T(128)} %bitcast.6, s32[8]{0:T(128)} %slab_hbm.1, ...), custom_call_target="tpu_custom_call" | custom-call | tf_op jit(solution)/shard_map/pallas_call | solution.py:298
  22.5 1.3 %shard_map.56 = f32[16,64,512]{2,1,0:T(8,128)} custom-call(f32[16,64,512]{2,1,0:T(8,128)S(1)} %get-tuple-element.10.done_ref, bf16[576,512]{1,0:T(8,128)(2,1)S(1)} %get-tuple-element.11.rows_ref, bf16[512,512]{1,0:T(8,128)(2,1)S(1)} %get-tuple-element.12.every_ref, s32[64,512]{1,0:T(8,128)S(1)} %get-tuple-element.13.labels_ref, ...), custom_call_target="tpu_custom_call" | custom-call | tf_op jit(solution)/shard_map/pallas_call | solution.py:332

commit v8 on v7

--- a/solution.py
+++ b/solution.py
@@ -206,7 +206,6 @@
     start_near("pw", pair_w, 0)
     start_far("pw", pair_w, 1)
     start_near("pw", pair_w, 1)
-    start_own("pw", pair_w, whole)
     slab_start("sw", slab_w, NEAR)
 
     loads[3].wait()
@@ -221,6 +220,7 @@
             part[at, :, chunk] = merged(wrap(y, step, NY), chunk)
             send(("ring", chunk), part.at[at, :, chunk], from_ring.at[at, :, chunk], ("y", step))
     slab_start("sw", slab_w, (2,))
+    start_own("pw", pair_w, whole)
 
     def ring_end(chunk):
         total = merged(y, chunk)

time: 24.1 us -> 23.9 us (level)
  no operation moved by 1% of the time
where the time goes in v8:
time: 23.9 us; the launch traced here: 23.8 us
  Pallas kernels  23.8 us (100%)
    pallas_call x1, Pallas kernels, local(): pl.pallas_call(kernel, out_shape=(jax.ShapeDtypeStruct((NJ, TILE, V), F32...  22.5 us
    pallas_call x1, Pallas kernels, local(): pl.pallas_call(finish, out_shape=jax.ShapeDtypeStruct((NJ, TILE, V), F32)...  1.34 us

profile of v8, /device:TPU:0, one launch (start us, length us, event | category | flops | bytes accessed | tf_op | source)
XLA Modules:
  0.0 23.8 jit_solution(199482163041541654)
XLA Ops:
  0.0 22.5 %shard_map.55 = (f32[16,64,512]{2,1,0:T(8,128)S(1)}, bf16[576,512]{1,0:T(8,128)(2,1)S(1)}, bf16[512,512]{1,0:T(8,128)(2,1)S(1)}, s32[64,512]{1,0:T(8,128)S(1)}, s32[16,128]{1,0:T(8,128)S(1)}) custom-call(bf16[4,2,2,2,16,512]{5,4,3,2,1,0:T(8,128)(2,1)} %bitcast.4, bf16[8,1,64,512]{3,2,1,0:T(8,128)(2,1)} %ints_hbm.1, s32[16]{0:T(128)} %bitcast.6, s32[8]{0:T(128)} %slab_hbm.1, ...), custom_call_target="tpu_custom_call" | custom-call | tf_op jit(solution)/shard_map/pallas_call | solution.py:298
  22.5 1.3 %shard_map.56 = f32[16,64,512]{2,1,0:T(8,128)} custom-call(f32[16,64,512]{2,1,0:T(8,128)S(1)} %get-tuple-element.10.done_ref, bf16[576,512]{1,0:T(8,128)(2,1)S(1)} %get-tuple-element.11.rows_ref, bf16[512,512]{1,0:T(8,128)(2,1)S(1)} %get-tuple-element.12.every_ref, s32[64,512]{1,0:T(8,128)S(1)} %get-tuple-element.13.labels_ref, ...), custom_call_target="tpu_custom_call" | custom-call | tf_op jit(solution)/shard_map/pallas_call | solution.py:332

commit v9 on v8

--- a/solution.py
+++ b/solution.py
@@ -58,7 +58,7 @@
 
 def kernel(
     amps_hbm, ints_hbm, occ_hbm, slab_hbm, virt_hbm, out_ref, rows_ref, every_ref, labels_ref, late_ref,
-    amps, ints, occ_ref, slab_ref, virt_ref, row_labels, from_sibling, part, from_ring,
+    amps, ints, occ_ref, slab_ref, virt_ref, row_labels, to_sibling, from_sibling, part, from_ring,
     pair_w, pair_a, slab_w, slab_a, spent, load_sems, send_sems, recv_sems,
 ):
     pair, slab = lax.axis_index("pair"), lax.axis_index("slab")
@@ -86,6 +86,7 @@
             (slab_hbm, slab_ref),
             (amps_hbm.at[:, core], amps),
             (ints_hbm.at[:, 0], ints),
+            (amps_hbm.at[:, sibling_core], to_sibling),
         ))
     ]
 
@@ -111,10 +112,6 @@
 
     def arrive(group, like):
         copy(group, like, like, "sibling").wait_recv()
-
-    pl.semaphore_wait(barrier, len(device))
-    for chunk in range(2):
-        send(("merge", chunk), amps_hbm.at[:, sibling_core, :, chunk], from_sibling.at[:, :, chunk], "sibling")
 
     for load in loads[:3]:
         load.wait()
@@ -200,6 +197,11 @@
 
     def slab_end(tag, buf):
         arrive((tag, "sibling"), buf.at[pl.ds(0, NY)])
+
+    loads[5].wait()
+    pl.semaphore_wait(barrier, len(device))
+    for chunk in range(2):
+        send(("merge", chunk), to_sibling.at[:, :, chunk], from_sibling.at[:, :, chunk], "sibling")
 
     whole = pl.ds(0, 2)
     start_far("pw", pair_w, 0)
@@ -314,6 +316,7 @@
                 pltpu.VMEM((1, V), jnp.int32),
                 pltpu.VMEM((V, 128), jnp.int32),
                 pltpu.VMEM((NY, *piece), BF16),
+                pltpu.VMEM((NY, *piece), BF16),
                 pltpu.VMEM((3, *piece), BF16),
                 pltpu.VMEM((3, *piece), BF16),
                 pltpu.VMEM((NJ, *piece), BF16),
@@ -321,7 +324,7 @@
                 pltpu.VMEM((NS, *piece), BF16),
                 pltpu.VMEM((NS, *piece), BF16),
                 pltpu.VMEM((N_SENT, 16, V), BF16),
-                pltpu.SemaphoreType.DMA((5,)),
+                pltpu.SemaphoreType.DMA((6,)),
                 pltpu.SemaphoreType.DMA((1,)),
                 pltpu.SemaphoreType.DMA((N_SEMS,)),
             ],

time: 23.9 us -> 23.7 us (level)
  no operation moved by 1% of the time
where the time goes in v9:
time: 23.7 us; the launch traced here: 23.6 us
  Pallas kernels  23.6 us (100%)
    pallas_call x1, Pallas kernels, local(): pl.pallas_call(kernel, out_shape=(jax.ShapeDtypeStruct((NJ, TILE, V), F32...  22.3 us
    pallas_call x1, Pallas kernels, local(): pl.pallas_call(finish, out_shape=jax.ShapeDtypeStruct((NJ, TILE, V), F32)...  1.34 us

profile of v9, /device:TPU:0, one launch (start us, length us, event | category | flops | bytes accessed | tf_op | source)
XLA Modules:
  0.0 23.6 jit_solution(2292470967583018531)
XLA Ops:
  0.0 22.3 %shard_map.55 = (f32[16,64,512]{2,1,0:T(8,128)S(1)}, bf16[576,512]{1,0:T(8,128)(2,1)S(1)}, bf16[512,512]{1,0:T(8,128)(2,1)S(1)}, s32[64,512]{1,0:T(8,128)S(1)}, s32[16,128]{1,0:T(8,128)S(1)}) custom-call(bf16[4,2,2,2,16,512]{5,4,3,2,1,0:T(8,128)(2,1)} %bitcast.4, bf16[8,1,64,512]{3,2,1,0:T(8,128)(2,1)} %ints_hbm.1, s32[16]{0:T(128)} %bitcast.6, s32[8]{0:T(128)} %slab_hbm.1, ...), custom_call_target="tpu_custom_call" | custom-call | tf_op jit(solution)/shard_map/pallas_call | solution.py:300
  22.3 1.3 %shard_map.56 = f32[16,64,512]{2,1,0:T(8,128)} custom-call(f32[16,64,512]{2,1,0:T(8,128)S(1)} %get-tuple-element.10.done_ref, bf16[576,512]{1,0:T(8,128)(2,1)S(1)} %get-tuple-element.11.rows_ref, bf16[512,512]{1,0:T(8,128)(2,1)S(1)} %get-tuple-element.12.every_ref, s32[64,512]{1,0:T(8,128)S(1)} %get-tuple-element.13.labels_ref, ...), custom_call_target="tpu_custom_call" | custom-call | tf_op jit(solution)/shard_map/pallas_call | solution.py:335

commit v10 on v9

--- a/solution.py
+++ b/solution.py
@@ -184,9 +184,10 @@
     def pair_far(tag, buf):
         arrive((tag, "far"), buf.at[pl.ds(0, 5)])
 
-    def slab_start(tag, buf, steps):
+    def slab_start(tag, buf, steps, chunk=slice(None)):
+        own = buf.at[slab, :, chunk]
         for step in steps:
-            send((tag, step), buf.at[slab], buf.at[slab], ("y", step))
+            send((tag, step), own, own, ("y", step))
 
     def slab_over(tag, buf):
         send((tag, "sibling"), buf.at[slab], buf.at[slab], "sibling")
@@ -239,12 +240,13 @@
     ring_end(0)
     start_far("pa", pair_a, 0)
     start_near("pa", pair_a, 0)
+    slab_start("sa", slab_a, STEPS, 0)
     ring_end(1)
     start_far("pa", pair_a, 1)
     start_near("pa", pair_a, 1)
+    slab_start("sa", slab_a, STEPS, 1)
     start_own("pa", pair_a, 0)
     start_own("pa", pair_a, 1)
-    slab_start("sa", slab_a, STEPS)
     turn_far("pa", pair_a, 0)
     turn_near("pa", pair_a, 0)
     slab_over("sw", slab_w)

time: 23.7 us -> 23.7 us (level)
  no operation moved by 1% of the time
where the time goes in v10:
time: 23.7 us; the launch traced here: 23.6 us
  Pallas kernels  23.6 us (100%)
    pallas_call x1, Pallas kernels, local(): pl.pallas_call(kernel, out_shape=(jax.ShapeDtypeStruct((NJ, TILE, V), F32...  22.3 us
    pallas_call x1, Pallas kernels, local(): pl.pallas_call(finish, out_shape=jax.ShapeDtypeStruct((NJ, TILE, V), F32)...  1.34 us

profile of v10, /device:TPU:0, one launch (start us, length us, event | category | flops | bytes accessed | tf_op | source)
XLA Modules:
  0.0 23.6 jit_solution(9453210024546932246)
XLA Ops:
  0.0 22.3 %shard_map.55 = (f32[16,64,512]{2,1,0:T(8,128)S(1)}, bf16[576,512]{1,0:T(8,128)(2,1)S(1)}, bf16[512,512]{1,0:T(8,128)(2,1)S(1)}, s32[64,512]{1,0:T(8,128)S(1)}, s32[16,128]{1,0:T(8,128)S(1)}) custom-call(bf16[4,2,2,2,16,512]{5,4,3,2,1,0:T(8,128)(2,1)} %bitcast.4, bf16[8,1,64,512]{3,2,1,0:T(8,128)(2,1)} %ints_hbm.1, s32[16]{0:T(128)} %bitcast.6, s32[8]{0:T(128)} %slab_hbm.1, ...), custom_call_target="tpu_custom_call" | custom-call | tf_op jit(solution)/shard_map/pallas_call | solution.py:302
  22.3 1.3 %shard_map.56 = f32[16,64,512]{2,1,0:T(8,128)} custom-call(f32[16,64,512]{2,1,0:T(8,128)S(1)} %get-tuple-element.10.done_ref, bf16[576,512]{1,0:T(8,128)(2,1)S(1)} %get-tuple-element.11.rows_ref, bf16[512,512]{1,0:T(8,128)(2,1)S(1)} %get-tuple-element.12.every_ref, s32[64,512]{1,0:T(8,128)S(1)} %get-tuple-element.13.labels_ref, ...), custom_call_target="tpu_custom_call" | custom-call | tf_op jit(solution)/shard_map/pallas_call | solution.py:337

commit v11 on v9

--- a/solution.py
+++ b/solution.py
@@ -126,7 +126,11 @@
 
     own_label = occ_ref[pair]
     amps_label = own_label ^ slab_ref[slab]
-    sibling_label = own_label ^ slab_ref[at_slab(0, False)]
+
+    def allowed(rows, of_core):
+        for at in range(NY):
+            labels = pair_labels(2 * at + of_core).reshape(2, 2, 16, V)
+            rows[at] = jnp.where(labels == amps_label, rows[at].astype(F32), 0.0).astype(BF16)
 
     loads[4].wait()
     wanted = pair_labels(slab) ^ own_label
@@ -199,6 +203,9 @@
         arrive((tag, "sibling"), buf.at[pl.ds(0, NY)])
 
     loads[5].wait()
+    allowed(to_sibling, sibling_core)
+    loads[3].wait()
+    allowed(amps, core)
     pl.semaphore_wait(barrier, len(device))
     for chunk in range(2):
         send(("merge", chunk), to_sibling.at[:, :, chunk], from_sibling.at[:, :, chunk], "sibling")
@@ -210,15 +217,12 @@
     start_near("pw", pair_w, 1)
     slab_start("sw", slab_w, NEAR)
 
-    loads[3].wait()
     def merged(at, chunk):
-        labels = pair_labels(2 * at + core).reshape(2, 2, 16, V)[:, chunk]
-        other = jnp.where(labels == sibling_label, from_sibling[at, :, chunk].astype(F32), 0.0)
-        return jnp.where(labels == amps_label, amps[at, :, chunk].astype(F32), other).astype(BF16)
+        return amps[at, :, chunk] + from_sibling[at, :, chunk]
 
     for chunk in range(2):
         arrive(("merge", chunk), from_sibling.at[:, :, chunk])
-        for at, step in enumerate(STEPS):
+        for at, step in enumerate((2, 1, -1)):
             part[at, :, chunk] = merged(wrap(y, step, NY), chunk)
             send(("ring", chunk), part.at[at, :, chunk], from_ring.at[at, :, chunk], ("y", step))
     slab_start("sw", slab_w, (2,))

time: 23.7 us -> 23.7 us (level)
  no operation moved by 1% of the time
where the time goes in v11:
time: 23.7 us; the launch traced here: 23.6 us
  Pallas kernels  23.5 us (99%)
    pallas_call x1, Pallas kernels, local(): pl.pallas_call(kernel, out_shape=(jax.ShapeDtypeStruct((NJ, TILE, V), F32...  22.2 us
    pallas_call x1, Pallas kernels, local(): pl.pallas_call(finish, out_shape=jax.ShapeDtypeStruct((NJ, TILE, V), F32)...  1.34 us

profile of v11, /device:TPU:0, one launch (start us, length us, event | category | flops | bytes accessed | tf_op | source)
XLA Modules:
  0.0 23.6 jit_solution(7674096789869407633)
XLA Ops:
  0.0 22.2 %shard_map.55 = (f32[16,64,512]{2,1,0:T(8,128)S(1)}, bf16[576,512]{1,0:T(8,128)(2,1)S(1)}, bf16[512,512]{1,0:T(8,128)(2,1)S(1)}, s32[64,512]{1,0:T(8,128)S(1)}, s32[16,128]{1,0:T(8,128)S(1)}) custom-call(bf16[4,2,2,2,16,512]{5,4,3,2,1,0:T(8,128)(2,1)} %bitcast.4, bf16[8,1,64,512]{3,2,1,0:T(8,128)(2,1)} %ints_hbm.1, s32[16]{0:T(128)} %bitcast.6, s32[8]{0:T(128)} %slab_hbm.1, ...), custom_call_target="tpu_custom_call" | custom-call | tf_op jit(solution)/shard_map/pallas_call | solution.py:304
  22.2 1.3 %shard_map.56 = f32[16,64,512]{2,1,0:T(8,128)} custom-call(f32[16,64,512]{2,1,0:T(8,128)S(1)} %get-tuple-element.10.done_ref, bf16[576,512]{1,0:T(8,128)(2,1)S(1)} %get-tuple-element.11.rows_ref, bf16[512,512]{1,0:T(8,128)(2,1)S(1)} %get-tuple-element.12.every_ref, s32[64,512]{1,0:T(8,128)S(1)} %get-tuple-element.13.labels_ref, ...), custom_call_target="tpu_custom_call" | custom-call | tf_op jit(solution)/shard_map/pallas_call | solution.py:339

commit v12 on v9

--- a/solution.py
+++ b/solution.py
@@ -10,7 +10,7 @@
 NS = 8
 TILE = 64
 V = 512
-N_SEMS = 26
+N_SEMS = 22
 N_SENT = 204
 NEAR = (1, -1)
 STEPS = (1, -1, 2)
@@ -186,13 +186,13 @@
 
     def slab_start(tag, buf, steps):
         for step in steps:
-            send((tag, step), buf.at[slab], buf.at[slab], ("y", step))
+            send((tag, "y"), buf.at[slab], buf.at[slab], ("y", step))
 
     def slab_over(tag, buf):
         send((tag, "sibling"), buf.at[slab], buf.at[slab], "sibling")
+        arrive((tag, "y"), buf.at[pl.ds(0, len(STEPS))])
         for step in STEPS:
             piece = buf.at[at_slab(-step)]
-            arrive((tag, step), piece)
             send((tag, "sibling"), piece, piece, "sibling")
 
     def slab_end(tag, buf):

time: 23.7 us -> 23.7 us (level)
  no operation moved by 1% of the time
where the time goes in v12:
time: 23.7 us; the launch traced here: 23.6 us
  Pallas kernels  23.6 us (100%)
    pallas_call x1, Pallas kernels, local(): pl.pallas_call(kernel, out_shape=(jax.ShapeDtypeStruct((NJ, TILE, V), F32...  22.2 us
    pallas_call x1, Pallas kernels, local(): pl.pallas_call(finish, out_shape=jax.ShapeDtypeStruct((NJ, TILE, V), F32)...  1.34 us

profile of v12, /device:TPU:0, one launch (start us, length us, event | category | flops | bytes accessed | tf_op | source)
XLA Modules:
  0.0 23.6 jit_solution(2135403621819950500)
XLA Ops:
  0.0 22.2 %shard_map.55 = (f32[16,64,512]{2,1,0:T(8,128)S(1)}, bf16[576,512]{1,0:T(8,128)(2,1)S(1)}, bf16[512,512]{1,0:T(8,128)(2,1)S(1)}, s32[64,512]{1,0:T(8,128)S(1)}, s32[16,128]{1,0:T(8,128)S(1)}) custom-call(bf16[4,2,2,2,16,512]{5,4,3,2,1,0:T(8,128)(2,1)} %bitcast.4, bf16[8,1,64,512]{3,2,1,0:T(8,128)(2,1)} %ints_hbm.1, s32[16]{0:T(128)} %bitcast.6, s32[8]{0:T(128)} %slab_hbm.1, ...), custom_call_target="tpu_custom_call" | custom-call | tf_op jit(solution)/shard_map/pallas_call | solution.py:300
  22.2 1.3 %shard_map.56 = f32[16,64,512]{2,1,0:T(8,128)} custom-call(f32[16,64,512]{2,1,0:T(8,128)S(1)} %get-tuple-element.10.done_ref, bf16[576,512]{1,0:T(8,128)(2,1)S(1)} %get-tuple-element.11.rows_ref, bf16[512,512]{1,0:T(8,128)(2,1)S(1)} %get-tuple-element.12.every_ref, s32[64,512]{1,0:T(8,128)S(1)} %get-tuple-element.13.labels_ref, ...), custom_call_target="tpu_custom_call" | custom-call | tf_op jit(solution)/shard_map/pallas_call | solution.py:335
